TPU v7x, 256 devices: a whole 4x4x8 slice. The times are simulated.
256 devices in a mesh: dp: 16 (over z_lo, x), fsdp: 16 (over y, z_hi, core).
Axes of the slice: x: 4, y: 4, z: 8 (z_hi: 2, z_lo: 4; z = z_hi * 4 + z_lo), core: 2. Of those that a mesh axis runs over, the one named last changes fastest.
Arguments:
- hidden: bfloat16 [131072, 4096], P(('dp', 'fsdp')), may hold values from -6 to 6
- temporal_gain: float32 [4096], replicated, may hold values from 0.1 to 1.9
- in_weight: bfloat16 [4096, 1024], P('fsdp'), may hold values from -0.09375 to 0.09375
- in_scale: bfloat16 [4096], P('fsdp'), may hold values from 0.25 to 4
- depth_gain: float32 [1024], replicated, may hold values from 0.1 to 1.9
- head_weight: bfloat16 [4, 1024, 1024], P(None, 'fsdp'), may hold values from -0.625 to 0.625
- code_ids: int32 [131072, 4], P(('dp', 'fsdp')), may hold values from 0 to 1023
Outputs:
- frame_loss: float32 [131072, 4], P(('dp', 'fsdp'))
- head_grad: float32 [4, 1024, 1024], P(None, 'fsdp')
All inputs are finite; a program needn't handle non-finite values.
Results may differ from a plain program's by a relative error of at most 0.0043.
Values may be sent and summed in bfloat16 or wider, within the bound.
A program may use at most 128 MiB of HBM per device.

v0:
```python
import jax
import jax.numpy as jnp
from jax import lax
from jax.sharding import PartitionSpec as P

epsilon = 1e-05
softcap = 30.0
loss_scale = 0.0625


def shards(hidden, temporal_gain, in_weight, in_scale, depth_gain, head_weight, code_ids):
    frames = hidden.shape[0]
    row_block = hidden.astype(jnp.float32)
    normed = (
        row_block
        * lax.rsqrt(jnp.mean(row_block * row_block, axis=-1, keepdims=True) + epsilon)
        * temporal_gain
    ).astype(jnp.bfloat16)
    stored = lax.all_gather(in_weight, "fsdp", axis=0, tiled=True)
    row_scale = lax.all_gather(in_scale, "fsdp", axis=0, tiled=True)
    dequant = (stored.astype(jnp.float32) * row_scale.astype(jnp.float32)[:, None]).astype(
        jnp.bfloat16
    )
    depth_in = jnp.dot(normed, dequant, preferred_element_type=jnp.float32)
    depth_rows = (
        depth_in
        * lax.rsqrt(jnp.mean(depth_in * depth_in, axis=-1, keepdims=True) + epsilon)
        * depth_gain
    ).astype(jnp.bfloat16)
    card_count = head_weight.shape[1]
    group_rows = lax.all_gather(depth_rows, "fsdp", axis=0, tiled=True)
    group_ids = lax.all_gather(code_ids, "fsdp", axis=0, tiled=True)
    scores = jnp.einsum("rd,kcd->rkc", group_rows, head_weight, preferred_element_type=jnp.float32)
    capped = softcap * jnp.tanh(scores / softcap)
    offset = lax.axis_index("fsdp") * card_count
    card_iota = lax.broadcasted_iota(jnp.int32, (1, 1, card_count), 2)
    onehot = ((group_ids - offset)[:, :, None] == card_iota).astype(jnp.float32)
    exp_sums = jnp.sum(jnp.exp(capped), axis=2)
    target = jnp.sum(onehot * capped, axis=2)
    totals, targets = lax.psum((exp_sums, target), "fsdp")
    log_total = jnp.log(totals)
    losses = log_total - targets
    own_loss = lax.dynamic_slice_in_dim(losses, lax.axis_index("fsdp") * frames, frames, 0)
    prob_rows = jnp.exp(capped - log_total[:, :, None])
    dlogits = ((prob_rows - onehot) * (1.0 - (capped / softcap) ** 2) * loss_scale).astype(
        jnp.bfloat16
    )
    grad_part = jnp.einsum("rkc,rd->kcd", dlogits, group_rows, preferred_element_type=jnp.float32)
    head_grad = lax.psum(grad_part, "dp")
    return (own_loss, head_grad)


def solution(mesh):
    in_specs = (
        P(("dp", "fsdp"), None),
        P(),
        P("fsdp", None),
        P("fsdp"),
        P(),
        P(None, "fsdp", None),
        P(("dp", "fsdp"), None),
    )
    out_specs = (P(("dp", "fsdp"), None), P(None, "fsdp", None))
    return jax.shard_map(shards, mesh=mesh, in_specs=in_specs, out_specs=out_specs, check_vma=False)
```

profile of v0, /device:TPU:2, one launch (start us, length us, event | category | flops | bytes accessed | tf_op | source)
XLA Modules:
  0.0 676.1 jit_solution(2911526151780255984)
XLA Ops:
  7.2 0.0 copy-start
  7.2 0.0 all-gather.4.cloned.1.call-start
  7.2 0.7 all-gather.4.cloned.1.call-update
  7.9 0.0 all-gather.6.cloned.1.call-start
  8.0 0.7 reshape.25
  8.6 35.2 %all-gather = bf16[16,1,256]{2,1,0:T(2,128)(2,1)S(1)} all-gather(bf16[1,1,256]{2,1,0:T(2,128)(2,1)S(1)} %reshape.25), channel_id=1, replica_groups=mesh['dp'=16,'fsdp'=16] {'fsdp'}, dimensions={0}, use_global_device_ids=true | all-gather | bytes 8704 | tf_op jit(solution)/shard_map/all_gather | solution.py:20
  43.8 3.1 fusion.10
  46.9 75.1 %all-gather.4.cloned.1.call-done = bf16[4096,1024]{1,0:T(8,128)(2,1)} async-done(((bf16[256,1024]{1,0:T(8,128)(2,1)}), bf16[4096,1024]{1,0:T(8,128)(2,1)}) %all-gather.4.cloned.1.call-update) | async-done | bytes 8388624 | tf_op jit(solution)/shard_map/all_gather | solution.py:19
  122.0 0.0 copy-start.2
  122.0 0.0 copy-start.1
  122.0 9.4 %multiply_reduce_fusion = (f32[512]{0:T(512)S(1)}, f32[512,1024]{1,0:T(8,128)S(1)}) fusion(bf16[4096,1024]{1,0:T(8,128)(2,1)} %all-gather.4.cloned.1.call-done, f32[4096]{0:T(1024)S(1)} %bitcast.13, bf16[512,4096]{1,0:T(8,128)(2,1)} %param.7, f32[4096]{0:T(1024)} %param.8, f32[512]{0:T(512)S(1)} %add_rsqrt_fusion.1), kind=kOutput, calls=%fused_computation.26 | convolution fusion | flops 4316986880 | bytes 14716928 | tf_op jit(solution)/shard_map/dot_general | solution.py:24
  131.4 0.0 copy-done.2
  131.4 1.2 multiply_convert_fusion.4
  132.6 0.0 all-gather.6.cloned.1.call-update
  132.6 0.0 all-reduce.6.cloned.1.call-start
  132.7 0.0 copy-done.1
  132.7 25.9 %all_gather.15 = s32[8192,4]{0,1:T(4,128)S(1)} all-gather(s32[512,4]{0,1:T(4,128)S(1)} %copy-done.1), channel_id=1, replica_groups=mesh['dp'=16,'fsdp'=16] {'fsdp'}, dimensions={0}, use_global_device_ids=true | all-gather | bytes 139264 | tf_op jit(solution)/shard_map/all_gather | solution.py:32
  158.6 144.6 %all-gather.6.cloned.1.call-done = bf16[8192,1024]{1,0:T(8,128)(2,1)} async-done(((bf16[512,1024]{1,0:T(8,128)(2,1)}), bf16[8192,1024]{1,0:T(8,128)(2,1)}) %all-gather.6.cloned.1.call-update) | async-done | bytes 16777232 | tf_op jit(solution)/shard_map/all_gather | solution.py:31
  303.2 0.0 copy-done
  303.2 13.2 %exponential_reduce_fusion = (f32[8192,4]{0,1:T(4,128)}, f32[8192,4]{0,1:T(4,128)}, f32[8192,4,64]{0,2,1:T(8,128)}) fusion(s32[8192,4]{0,1:T(4,128)S(1)} %broadcast_subtract_fusion, bf16[4,64,1024]{2,1,0:T(8,128)(2,1)S(1)} %copy-done, bf16[8192,1024]{1,0:T(8,128)(2,1)} %all-gather.6.cloned.1.call-done), kind=kOutput, calls=%fused_computation.16 | convolution fusion | flops 4307484672 | bytes 26083328 | tf_op jit(solution)/shard_map/rd,kcd->rkc/dot_general | solution.py:33
  316.4 0.0 all-reduce.6.cloned.1.call-update
  316.4 0.2 all-reduce.4.cloned.1.call-start
  316.6 170.9 %all-reduce.6.cloned.1.call-done = (f32[8192,4]{0,1:T(4,128)}, f32[8192,4]{0,1:T(4,128)}) async-done(((f32[8192,4]{0,1:T(4,128)}, f32[8192,4]{0,1:T(4,128)}), (f32[8192,4]{0,1:T(4,128)}, f32[8192,4]{0,1:T(4,128)})) %all-reduce.6.cloned.1.call-update) | async-done | bytes 262160 | tf_op jit(solution)/shard_map/psum | solution.py:40
  487.5 0.9 log.3
  488.4 15.1 %fusion = f32[4,64,1024]{2,1,0:T(8,128)} fusion(bf16[8192,1024]{1,0:T(8,128)(2,1)} %all-gather.6.cloned.1.call-done, f32[8192,4,64]{0,2,1:T(8,128)} %get-tuple-element.8, f32[8192,4]{0,1:T(4,128)S(1)} %log.3, s32[8192,4]{0,1:T(4,128)S(1)} %broadcast_subtract_fusion), kind=kOutput, calls=%fused_computation | convolution fusion | flops 4315938816 | bytes 26476544 | tf_op jit(solution)/shard_map/rkc,rd->kcd/dot_general | solution.py:48
  503.5 0.0 all-reduce.4.cloned.1.call-update
  503.5 1.3 dynamic-slice_subtract_fusion
  504.8 162.4 %all-reduce.4.cloned.1.call-done = f32[4,64,1024]{2,1,0:T(8,128)} async-done(((f32[4,64,1024]{2,1,0:T(8,128)}), f32[4,64,1024]{2,1,0:T(8,128)}) %all-reduce.4.cloned.1.call-update) | async-done | bytes 1048592 | tf_op jit(solution)/shard_map/psum | solution.py:49
  667.3 2.3 copy.12
  (4 shorter events, 0.1 us)
Async XLA Ops:
  7.2 296.0 %copy-start = (bf16[4,64,1024]{2,1,0:T(8,128)(2,1)S(1)}, bf16[4,64,1024]{2,1,0:T(8,128)(2,1)}, u32[]{:S(2)}) copy-start(bf16[4,64,1024]{2,1,0:T(8,128)(2,1)} %param.12) | copy-start | bytes 1572868
  7.2 114.8 %all-gather.4.cloned.1.call-start = ((), (), s32[]{:S(2)}) async-start(), calls=%async_computation | async-start | bytes 8912896 | tf_op jit(solution)/shard_map/all_gather | solution.py:19
  7.9 295.3 %all-gather.6.cloned.1.call-start = ((), (), s32[]{:S(2)}) async-start(), calls=%async_computation.1 | async-start | bytes 17825792 | tf_op jit(solution)/shard_map/all_gather | solution.py:31
  122.0 9.4 %copy-start.2 = (f32[1024]{0:T(1024)S(1)}, f32[1024]{0:T(1024)}, u32[]{:S(2)}) copy-start(f32[1024]{0:T(1024)} %param.11) | copy-start | bytes 12292
  122.0 10.7 %copy-start.1 = (s32[512,4]{0,1:T(4,128)S(1)}, s32[512,4]{0,1:T(4,128)}, u32[]{:S(2)}) copy-start(s32[512,4]{0,1:T(4,128)} %param.13) | copy-start | bytes 24580
  132.6 354.9 %all-reduce.6.cloned.1.call-start = ((), (), s32[]{:S(2)}) async-start(), calls=%async_computation.3 | async-start | bytes 524288 | tf_op jit(solution)/shard_map/psum | solution.py:40
  316.4 350.8 %all-reduce.4.cloned.1.call-start = ((), (), s32[]{:S(2)}) async-start(), calls=%async_computation.2 | async-start | bytes 2097152 | tf_op jit(solution)/shard_map/psum | solution.py:49
Sparse Core Ops, SparseCore 0:
  10.7 111.2 all-gather.3
  132.7 170.3 all-gather.5
  316.5 170.9 all-reduce.5
  503.6 163.5 all-reduce.3
where the time goes:
time: 677 us; the launch traced here: 676 us
  waiting for transfers between devices  554 us (82%)
  blocking collectives  61.1 us (9%)
  matrix products  37.6 us (6%)
  between operations  13.8 us (2%)
    psum x1, waiting for transfers between devices, shards(): totals, targets = lax.psum((exp_sums, target), 'fsdp')  171 us
    psum x1, waiting for transfers between devices, shards(): head_grad = lax.psum(grad_part, 'dp')  162 us
    all_gather x1, waiting for transfers between devices, shards(): group_rows = lax.all_gather(depth_rows, 'fsdp', axis=0, tiled=True)  145 us
    all_gather x1, waiting for transfers between devices, shards(): stored = lax.all_gather(in_weight, 'fsdp', axis=0, tiled=True)  75.1 us
    all_gather x1, blocking collectives, shards(): row_scale = lax.all_gather(in_scale, 'fsdp', axis=0, tiled=True)  35.2 us
    all_gather x1, blocking collectives, shards(): group_ids = lax.all_gather(code_ids, 'fsdp', axis=0, tiled=True)  25.9 us
    dot_general x1, matrix products, shards(): jnp.einsum('rkc,rd->kcd', dlogits, group_rows, preferred_element_type=jnp...  15.1 us
  transfers between devices with their start and end apart: 4, of which 4 were waited for; matrix products, arithmetic and copies ran while one was open for 1% of the time, Pallas kernels for 0%

commit v1 on v0

v1 whole, which is shorter than its diff:
```python
import functools

import jax
import jax.numpy as jnp
from jax import lax
from jax.experimental import pallas as pl
from jax.experimental.pallas import tpu as pltpu
from jax.sharding import PartitionSpec as P

MESH = pl.DeviceIdType.MESH
f32, bf16 = jnp.float32, jnp.bfloat16
eps = 1e-05
cap = 30.0
loss_scale = 0.0625

Y_A, Y_B, Y_C, Y2, ZU, ZD, XQ = 0, 2, 4, 6, 8, 12, 16
GATHER = 26
SIB_W, SIB_R, SIB_S, SIB_I = 52, 60, 61, 62
A2, A1M, A1A, B2, B1M, B1A, S2A, S2B, S3, GZ, GX = 63, 71, 79, 87, 89, 91, 93, 96, 99, 106, 109
N_SEM = 112


def kernel(
    hidden, t_gain, weight, scale, d_gain, heads, ids,
    loss_out, grad_out,
    hid, normed, wg, hg, acc, rows, tb, eb, dl, gb,
    ra2, ra1m, ra1a, saa, rb2, rb1m, rb1a, sab, sa, sb, s2a, r2a, s2b, r2b, tt, s3, r3, fin,
    idb, sums, lsem, ss, rs,
):
    dp, fs = lax.axis_index("dp"), lax.axis_index("fsdp")
    x, y, c = dp % 4, fs // 4, fs % 2
    h, j = (fs // 2) % 2, dp // 4
    z = h * 4 + j
    par = x % 2

    def dev(px, py, pz, pc=None):
        px, py, pz = (px + 4) % 4, (py + 4) % 4, (pz + 8) % 8
        return {"dp": (pz % 4) * 4 + px, "fsdp": (py * 2 + pz // 4) * 2 + (c if pc is None else pc)}

    sib = dev(x, y, z, 1 - c)
    xd = lambda d: dev(x + d, y, z)
    yd = lambda d: dev(x, y + d, z)
    zd = lambda d: dev(x, y, z + d)

    def copy(src, dst, sem, to):
        return pltpu.make_async_remote_copy(
            src_ref=src, dst_ref=dst, send_sem=ss.at[sem], recv_sem=rs.at[sem], device_id=to, device_id_type=MESH
        )

    hid_copy = pltpu.make_async_copy(hidden, hid, lsem.at[0])
    hid_copy.start()
    own = y * 2 + h
    head_copy = pltpu.make_async_copy(heads, hg.at[own], lsem.at[1])
    head_copy.start()

    barrier = pltpu.get_barrier_semaphore()
    everyone = [sib] + [xd(d) for d in (1, 2, 3)] + [yd(d) for d in (1, 2, 3)] + [zd(d) for d in range(1, 8)]
    for to in everyone:
        pl.semaphore_signal(barrier, inc=1, device_id=to, device_id_type=MESH)

    mine = pl.ds(pl.multiple_of(c * 256, 256), 256)
    wg[own, mine, :] = (weight[...].astype(f32) * scale[...].astype(f32)).astype(bf16)
    idb[pl.ds(c, 1)] = ids[...][None]
    pl.semaphore_wait(barrier, len(everyone))

    def slot(role):
        off = jnp.where(role % 4 == 1, 3, jnp.where(role % 4 == 2, 1, jnp.where(role % 4 == 3, 2, 0)))
        return ((y + off) % 4) * 2 + jnp.where(role < 4, h, 1 - h)

    def piece(m, role, start, count):
        if m == 0:
            return wg.at[slot(role), pl.ds(pl.multiple_of(c * 256 + start, 64), count)]
        return hg.at[slot(role), pl.ds(pl.multiple_of(start, 64), count)]

    q0, q1, rest = par * 128, par * 128 + 64, (1 - par) * 128
    o0, o1 = (1 - par) * 128, (1 - par) * 128 + 64

    def move(m, role, start, count, sem, to):
        ref = piece(m, role, start, count)
        return copy(ref, ref, m * GATHER + sem, to)

    def y_sends(m):
        for sem, plus, minus, count in ((Y_A, q0, q1, 64), (Y_B, q1, q0, 64), (Y_C, rest, rest, 128)):
            move(m, 0, plus, count, sem, yd(1)).start()
            move(m, 0, minus, count, sem + 1, yd(-1)).start()

    def z_source(m, k):
        @pl.when(j == 3)
        def _():
            move(m, k, q0, 64, ZU + k, zd(1)).start()

        @pl.when(j == 0)
        def _():
            move(m, k, q1, 64, ZD + k, zd(-1)).start()

    def y_quarters(m):
        move(m, 1, q0, 64, Y_A, yd(1)).wait_recv()
        move(m, 1, q0, 64, Y2, yd(1)).start()
        move(m, 2, q1, 64, Y_A + 1, yd(-1)).wait_recv()
        move(m, 2, q1, 64, Y2 + 1, yd(-1)).start()
        move(m, 1, q1, 64, Y_B, yd(1)).wait_recv()
        z_source(m, 1)
        move(m, 2, q0, 64, Y_B + 1, yd(-1)).wait_recv()
        z_source(m, 2)

    def y_rest(m):
        move(m, 1, rest, 128, Y_C, yd(1)).wait_recv()
        move(m, 2, rest, 128, Y_C + 1, yd(-1)).wait_recv()

    def x_sends(m, role):
        move(m, role, q0, 64, XQ + 2 * (role - 3), xd(1)).start()
        move(m, role, q1, 64, XQ + 2 * (role - 3) + 1, xd(-1)).start()

    def y_far(m):
        move(m, 3, q0, 64, Y2, yd(1)).wait_recv()
        move(m, 3, q1, 64, Y2 + 1, yd(-1)).wait_recv()
        x_sends(m, 3)
        z_source(m, 3)

    def z_pass(m, k):
        move(m, 4 + k, q0, 64, ZU + k, zd(1)).wait_recv()

        @pl.when(j < 3)
        def _():
            move(m, 4 + k, q0, 64, ZU + k, zd(1)).start()

        move(m, 4 + k, q1, 64, ZD + k, zd(-1)).wait_recv()

        @pl.when(j > 0)
        def _():
            move(m, 4 + k, q1, 64, ZD + k, zd(-1)).start()

        x_sends(m, 4 + k)

    def x_wait(m, role):
        sem = XQ + 2 * (role - 3)
        move(m, role, o0, 64, sem, xd(1)).wait_recv()
        move(m, role, o1, 64, sem + 1, xd(-1)).wait_recv()

    def to_sibling(role):
        ref = wg.at[slot(role), mine]
        return copy(ref, ref, SIB_W + role, sib)

    theirs = pl.ds(pl.multiple_of((1 - c) * 256, 256), 256)

    def project(role):
        ref = wg.at[slot(role), theirs]
        copy(ref, ref, SIB_W + role, sib).wait_recv()
        s = slot(role)

        @pl.loop(0, 4)
        def _(n):
            cols = pl.ds(pl.multiple_of(n * 256, 256), 256)
            acc[:, cols] += jnp.dot(normed[s], wg[s, :, cols], preferred_element_type=f32)

    to_sibling(0).start()
    y_sends(0)
    z_source(0, 0)
    id_copy = copy(idb.at[c], idb.at[c], SIB_I, sib)
    id_copy.start()
    hid_copy.wait()
    head_copy.wait()
    y_sends(1)
    z_source(1, 0)

    @pl.loop(0, 32)
    def _(r):
        at = pl.ds(pl.multiple_of(r * 16, 16), 16)
        block = hid[at, :].astype(f32)
        inv = lax.rsqrt(jnp.mean(block * block, axis=-1, keepdims=True) + eps)
        out = (block * inv * t_gain[...]).astype(bf16)
        for s in range(8):
            normed[s, at, :] = out[:, s * 512 : (s + 1) * 512]

    acc[...] = jnp.zeros_like(acc)
    y_quarters(0)
    z_pass(0, 0)
    y_far(0)
    y_quarters(1)
    z_pass(1, 0)
    z_pass(0, 1)
    z_pass(0, 2)
    y_far(1)
    y_rest(0)
    to_sibling(1).start()
    to_sibling(2).start()
    z_pass(0, 3)
    project(0)
    z_pass(1, 1)
    z_pass(1, 2)
    project(1)
    project(2)
    x_wait(0, 3)
    to_sibling(3).start()
    x_wait(0, 4)
    to_sibling(4).start()
    z_pass(1, 3)
    project(3)
    x_wait(0, 5)
    to_sibling(5).start()
    project(4)
    x_wait(0, 6)
    to_sibling(6).start()
    project(5)
    x_wait(0, 7)
    to_sibling(7).start()
    project(6)
    project(7)

    @pl.loop(0, 16)
    def _(r):
        at = pl.ds(pl.multiple_of(r * 32, 32), 32)
        block = acc[at, :]
        inv = lax.rsqrt(jnp.mean(block * block, axis=-1, keepdims=True) + eps)
        rows[pl.ds(pl.multiple_of(c * 512 + r * 32, 32), 32), :] = (block * inv * d_gain[...]).astype(bf16)

    my_rows = rows.at[pl.ds(pl.multiple_of(c * 512, 512), 512)]
    row_copy = copy(my_rows, my_rows, SIB_R, sib)
    sums[...] = jnp.zeros_like(sums)
    row_copy.start()
    id_copy.wait_recv()
    row_copy.wait_recv()
    y_rest(1)

    def score(role):
        s = slot(role)

        @pl.loop(0, 4)
        def _(n):
            cols = pl.ds(pl.multiple_of(n * 256, 256), 256)
            got = lax.dot_general(
                hg[s], rows[cols, :], (((1,), (1,)), ((), ())), preferred_element_type=f32
            )
            t = jnp.tanh(got * (1.0 / cap))
            e = jnp.exp(t * cap)
            tb[s, :, cols] = t
            eb[s, :, cols] = e
            ids_at = idb[n // 2, :, pl.ds(pl.multiple_of((n % 2) * 256, 256), 256)]
            card = lax.broadcasted_iota(jnp.int32, (64, 256), 0) + (s * 2 + c) * 64
            for k in range(4):
                part = slice(k * 64, (k + 1) * 64)
                hit = card == ids_at[k : k + 1, :]
                sums[c, k : k + 1, cols] += jnp.sum(e[part], axis=0, keepdims=True)
                sums[c, k + 4 : k + 5, cols] += jnp.sum(jnp.where(hit, t[part], 0.0), axis=0, keepdims=True)

    @pl.loop(0, 3)
    def _(role):
        score(role)

    @pl.loop(3, 8)
    def _(role):
        x_wait(1, role)
        score(role)

    my_sums = sums.at[c]
    sum_copy = copy(my_sums, my_sums, SIB_S, sib)
    sum_copy.start()
    sum_copy.wait_recv()
    totals = sums[0, 0:4, :] + sums[1, 0:4, :]
    mine_f = pl.ds(pl.multiple_of(c * 512, 512), 512)
    loss_out[...] = jnp.log(sums[0, 0:4, mine_f] + sums[1, 0:4, mine_f]) - cap * (
        sums[0, 4:8, mine_f] + sums[1, 4:8, mine_f]
    )
    sum_copy.wait_send()
    sums[c, 0:4, :] = 1.0 / totals

    def gradient(i):
        hp = i % 2
        s = 1 - 2 * hp
        step = i // 2
        off = jnp.where(step == 0, 2, jnp.where(step == 1, 4 - s, jnp.where(step == 2, 4 + s, 0)))
        b = ((y + off) % 4) * 2 + hp

        @pl.loop(0, 4)
        def _(n):
            cols = pl.ds(pl.multiple_of(n * 256, 256), 256)
            ids_at = idb[n // 2, :, pl.ds(pl.multiple_of((n % 2) * 256, 256), 256)]
            card = lax.broadcasted_iota(jnp.int32, (64, 256), 0) + (b * 2 + c) * 64
            for k in range(4):
                part = slice(k * 64, (k + 1) * 64)
                t = tb[b, part, cols]
                p = eb[b, part, cols] * sums[c, k : k + 1, cols]
                hit = card == ids_at[k : k + 1, :]
                p = jnp.where(hit, p - 1.0, p)
                dl[part, cols] = (p * ((1.0 - t * t) * loss_scale)).astype(bf16)

        @pl.loop(0, 4)
        def _(n):
            cols = pl.ds(pl.multiple_of(n * 256, 256), 256)
            g = jnp.dot(dl[...], rows[:, cols], preferred_element_type=f32)
            eb[b, :, cols] = g
            gb[b, :, cols] = g.astype(bf16)

        head = lambda d: pl.ds(pl.multiple_of(((x + d + 4) % 4) * 64, 64), 64)
        copy(gb.at[b, head(2), pl.ds(0, 512)], ra2.at[b], A2 + b, xd(s)).start()
        copy(gb.at[b, head(-s), pl.ds(0, 512)], ra1m.at[b], A1M + b, xd(-s)).start()

        @pl.when(step == 0)
        def _():
            copy(gb.at[b, :, pl.ds(512, 512)], rb2.at[hp], B2 + hp, yd(s)).start()

        @pl.when(step == 1)
        def _():
            copy(gb.at[b, :, pl.ds(512, 512)], rb1m.at[hp], B1M + hp, yd(-s)).start()

    @pl.loop(0, 8)
    def _(i):
        gradient(i)

    for hp in range(2):
        s = 1 - 2 * hp
        b = ((y + s + 4) % 4) * 2 + hp
        copy(sab.at[hp], rb2.at[hp], B2 + hp, yd(s)).wait_recv()
        for r in range(4):
            part = slice(r * 64, (r + 1) * 64)
            sab[hp, part, :] = (eb[b, part, 512:1024] + rb2[hp, part, :].astype(f32)).astype(bf16)
        copy(sab.at[hp], rb1a.at[hp], B1A + hp, yd(s)).start()

    @pl.loop(0, 8)
    def _(b):
        s = 1 - 2 * (b % 2)
        at = pl.ds(pl.multiple_of(((x + s + 4) % 4) * 64, 64), 64)
        copy(saa.at[b], ra2.at[b], A2 + b, xd(s)).wait_recv()
        saa[b] = (eb[b, at, 0:512] + ra2[b].astype(f32)).astype(bf16)
        copy(saa.at[b], ra1a.at[b], A1A + b, xd(s)).start()

    my_head = pl.ds(pl.multiple_of(x * 64, 64), 64)
    for hp in range(2):
        s = 1 - 2 * hp
        copy(sab.at[hp], rb1m.at[hp], B1M + hp, yd(-s)).wait_recv()
        copy(sab.at[hp], rb1a.at[hp], B1A + hp, yd(s)).wait_recv()
        for r in range(4):
            part = slice(r * 64, (r + 1) * 64)
            sb[hp, part, :] = (
                eb[y * 2 + hp, part, 512:1024] + rb1m[hp, part, :].astype(f32) + rb1a[hp, part, :].astype(f32)
            )
    for d in (2, 1, 3):
        at = pl.ds(pl.multiple_of(((x + d) % 4) * 64, 64), 64)
        s2b[d - 1] = sb[:, at, :].astype(bf16)
        copy(s2b.at[d - 1], r2b.at[d - 1], S2B + d - 1, xd(d)).start()

    @pl.loop(0, 8)
    def _(b):
        s = 1 - 2 * (b % 2)
        copy(saa.at[b], ra1m.at[b], A1M + b, xd(-s)).wait_recv()
        copy(saa.at[b], ra1a.at[b], A1A + b, xd(s)).wait_recv()
        sa[b] = eb[b, my_head, 0:512] + ra1m[b].astype(f32) + ra1a[b].astype(f32)

    for d in (2, 1, 3):
        s2a[d - 1] = sa[pl.ds(((y + d) % 4) * 2, 2)].astype(bf16)
        copy(s2a.at[d - 1], r2a.at[d - 1], S2A + d - 1, yd(d)).start()

    for d in range(3):
        copy(s2b.at[d], r2b.at[d], S2B + d, xd(d + 1)).wait_recv()
    tt[:, :, 512:1024] = (
        sb[:, my_head, :] + r2b[0].astype(f32) + r2b[1].astype(f32) + r2b[2].astype(f32)
    )
    for d in range(3):
        copy(s2a.at[d], r2a.at[d], S2A + d, yd(d + 1)).wait_recv()
    tt[:, :, 0:512] = (
        sa[pl.ds(y * 2, 2)] + r2a[0].astype(f32) + r2a[1].astype(f32) + r2a[2].astype(f32)
    )
    s3[...] = tt[...].astype(bf16)
    for d in (4, 3, 5, 2, 6, 1, 7):
        to = (z + d) % 8
        at = pl.ds(pl.multiple_of((to % 4) * 16, 16), 16)
        copy(s3.at[to // 4, at], r3.at[d - 1], S3 + d - 1, zd(d)).start()
    strip = pl.ds(pl.multiple_of(j * 16, 16), 16)
    total = tt[h, strip, :]
    for d in (1, 7, 2, 6, 3, 5, 4):
        copy(r3.at[d - 1], r3.at[d - 1], S3 + d - 1, zd(d)).wait_recv()
        total = total + r3[d - 1].astype(f32)

    fin[x, strip, :] = total.astype(bf16)
    def z_share(d):
        to = h * 4 + (j + d) % 4
        return copy(fin.at[x, strip], fin.at[x, strip], GZ + d - 1, dev(x, y, to))
    for d in (2, 1, 3):
        z_share(d).start()
    for d in (1, 2, 3):
        z_share(d).wait_recv()
    def x_share(d):
        return copy(fin.at[x], fin.at[x], GX + d - 1, xd(d))
    for d in (2, 1, 3):
        x_share(d).start()
    grad_out[x] = fin[x].astype(f32)
    for d in (1, 3, 2):
        x_share(d).wait_recv()
        src = (x + 4 - d) % 4
        grad_out[src] = fin[src].astype(f32)

    for m in range(2):
        for sem, count in ((Y_A, 64), (Y_A + 1, 64), (Y_B, 64), (Y_B + 1, 64), (Y_C, 128), (Y_C + 1, 128)):
            move(m, 0, 0, count, sem, yd(1)).wait_send()
        for sem in range(Y2, GATHER):
            move(m, 0, 0, 64, sem, yd(1)).wait_send()
    for role in range(8):
        to_sibling(role).wait_send()
    row_copy.wait_send()
    id_copy.wait_send()
    for b in range(8):
        for sem in (A2, A1M, A1A):
            copy(saa.at[b], ra2.at[b], sem + b, sib).wait_send()
    for hp in range(2):
        for sem in (B2, B1M, B1A):
            copy(sab.at[hp], rb2.at[hp], sem + hp, sib).wait_send()
    for d in range(3):
        copy(s2a.at[d], r2a.at[d], S2A + d, sib).wait_send()
        copy(s2b.at[d], r2b.at[d], S2B + d, sib).wait_send()
        z_share(d + 1).wait_send()
        x_share(d + 1).wait_send()
    for d in range(7):
        copy(r3.at[d], r3.at[d], S3 + d, sib).wait_send()


def shards(hidden, temporal_gain, in_weight, in_scale, depth_gain, head_weight, code_ids):
    vmem = pl.BlockSpec(memory_space=pltpu.VMEM)
    hbm = pl.BlockSpec(memory_space=pl.ANY)
    V = pltpu.VMEM
    loss, grad = pl.pallas_call(
        kernel,
        out_shape=(jax.ShapeDtypeStruct((4, 512), f32), jax.ShapeDtypeStruct((4, 64, 1024), f32)),
        in_specs=[hbm, vmem, vmem, vmem, vmem, hbm, vmem],
        out_specs=(vmem, vmem),
        scratch_shapes=[
            V((512, 4096), bf16), V((8, 512, 512), bf16), V((8, 512, 1024), bf16), V((8, 256, 1024), bf16),
            V((512, 1024), f32), V((1024, 1024), bf16), V((8, 256, 1024), f32), V((8, 256, 1024), f32),
            V((256, 1024), bf16), V((8, 256, 1024), bf16),
            V((8, 64, 512), bf16), V((8, 64, 512), bf16), V((8, 64, 512), bf16), V((8, 64, 512), bf16),
            V((2, 256, 512), bf16), V((2, 256, 512), bf16), V((2, 256, 512), bf16), V((2, 256, 512), bf16),
            V((8, 64, 512), f32), V((2, 256, 512), f32),
            V((3, 2, 64, 512), bf16), V((3, 2, 64, 512), bf16), V((3, 2, 64, 512), bf16), V((3, 2, 64, 512), bf16),
            V((2, 64, 1024), f32), V((2, 64, 1024), bf16), V((7, 16, 1024), bf16), V((4, 64, 1024), bf16),
            V((2, 4, 512), jnp.int32), V((2, 8, 1024), f32),
            pltpu.SemaphoreType.DMA((2,)), pltpu.SemaphoreType.DMA((N_SEM,)), pltpu.SemaphoreType.DMA((N_SEM,)),
        ],
        compiler_params=pltpu.CompilerParams(
            collective_id=0, has_side_effects=True, vmem_limit_bytes=63 * 2**20
        ),
    )(
        hidden, temporal_gain[None, :], in_weight, in_scale[:, None], depth_gain[None, :],
        head_weight.reshape(256, 1024), code_ids.T,
    )
    return loss.T, grad


def solution(mesh):
    in_specs = (
        P(("dp", "fsdp"), None),
        P(),
        P("fsdp", None),
        P("fsdp"),
        P(),
        P(None, "fsdp", None),
        P(("dp", "fsdp"), None),
    )
    out_specs = (P(("dp", "fsdp"), None), P(None, "fsdp", None))
    return jax.shard_map(shards, mesh=mesh, in_specs=in_specs, out_specs=out_specs, check_vma=False)
```

time: 677 us -> 297 us (0.44)
  waiting for transfers between devices: 554 us -> 0 us
  Pallas kernels: 0 us -> 290 us
  blocking collectives: 61.1 us -> 0 us
  matrix products: 37.6 us -> 0 us
  between operations: 13.8 us -> 0.64 us
    psum x2 -> x0, waiting for transfers between devices: 333 us -> none  [the longest x1 171 us: shards(): totals, targets = lax.psum((exp_sums, target), 'fsdp')]
    pallas_call x0 -> x1, Pallas kernels: none -> 290 us  [shards(): pl.pallas_call(kernel, out_shape=(jax.ShapeDtypeStruct((4, 512), f32), ja...]
    all_gather x2 -> x0, waiting for transfers between devices: 220 us -> none  [the longest x1 145 us: shards(): group_rows = lax.all_gather(depth_rows, 'fsdp', axis=0, tiled=True)]
    all_gather x2 -> x0, blocking collectives: 61.1 us -> none  [the longest x1 35.2 us: shards(): row_scale = lax.all_gather(in_scale, 'fsdp', axis=0, tiled=True)]
    dot_general x3 -> x0, matrix products: 37.6 us -> none  [the longest x1 15.1 us: shards(): jnp.einsum('rkc,rd->kcd', dlogits, group_rows, preferred_element_type=jnp...]
  transfers between devices with their start and end apart: 4 -> 0, of which waited for: 4 -> 0; matrix products, arithmetic and copies ran while one was open for 1% -> 0% of each run, Pallas kernels for 0% -> 0%
where the time goes in v1:
time: 297 us; the launch traced here: 295 us
  Pallas kernels  290 us (98%)
  local copies, waits for them, and re-layouts  4.99 us (2%)
    pallas_call x1, Pallas kernels, shards(): pl.pallas_call(kernel, out_shape=(jax.ShapeDtypeStruct((4, 512), f32), ja...  290 us

profile of v1, /device:TPU:2, one launch (start us, length us, event | category | flops | bytes accessed | tf_op | source)
XLA Modules:
  0.0 295.3 jit_solution(10940865241144837664)
XLA Ops:
  0.6 1.4 broadcast_in_dim.12.scale
  2.0 289.7 %shard_map.86 = (f32[4,512]{1,0:T(4,128)}, f32[4,64,1024]{2,1,0:T(8,128)}) custom-call(bf16[512,4096]{1,0:T(8,128)(2,1)} %hidden.1, f32[1,4096]{1,0:T(1,128)} %bitcast.6, bf16[256,1024]{1,0:T(8,128)(2,1)} %weight.1, bf16[256,1]{1,0:T(8,128)(2,1)} %broadcast_in_dim.12.scale, f32[1,1024]{1,0:T(1,128)} %bitcast.9, bf16[256,1024]{1,0:T(8,128)(2,1)} %bitcast.5, ...), custom_call_target="tpu_custom_call" | custom-call | tf_op jit(solution)/shard_map/pallas_call | solution.py:420
  291.7 1.3 copy.12
  293.0 2.3 copy.13

commit v2 on v1

--- a/solution.py
+++ b/solution.py
@@ -23,7 +23,7 @@
 def kernel(
     hidden, t_gain, weight, scale, d_gain, heads, ids,
     loss_out, grad_out,
-    hid, normed, wg, hg, acc, rows, tb, eb, dl, gb,
+    hid, normed, pg, ws, acc, rows, tb, eb, dl, gb,
     ra2, ra1m, ra1a, saa, rb2, rb1m, rb1a, sab, sa, sb, s2a, r2a, s2b, r2b, tt, s3, r3, fin,
     idb, sums, lsem, ss, rs,
 ):
@@ -50,7 +50,7 @@
     hid_copy = pltpu.make_async_copy(hidden, hid, lsem.at[0])
     hid_copy.start()
     own = y * 2 + h
-    head_copy = pltpu.make_async_copy(heads, hg.at[own], lsem.at[1])
+    head_copy = pltpu.make_async_copy(heads, pg.at[1, own], lsem.at[1])
     head_copy.start()
 
     barrier = pltpu.get_barrier_semaphore()
@@ -58,8 +58,7 @@
     for to in everyone:
         pl.semaphore_signal(barrier, inc=1, device_id=to, device_id_type=MESH)
 
-    mine = pl.ds(pl.multiple_of(c * 256, 256), 256)
-    wg[own, mine, :] = (weight[...].astype(f32) * scale[...].astype(f32)).astype(bf16)
+    pg[0, own] = (weight[...].astype(f32) * scale[...].astype(f32)).astype(bf16)
     idb[pl.ds(c, 1)] = ids[...][None]
     pl.semaphore_wait(barrier, len(everyone))
 
@@ -68,9 +67,7 @@
         return ((y + off) % 4) * 2 + jnp.where(role < 4, h, 1 - h)
 
     def piece(m, role, start, count):
-        if m == 0:
-            return wg.at[slot(role), pl.ds(pl.multiple_of(c * 256 + start, 64), count)]
-        return hg.at[slot(role), pl.ds(pl.multiple_of(start, 64), count)]
+        return pg.at[m, slot(role), pl.ds(pl.multiple_of(start, 64), count)]
 
     q0, q1, rest = par * 128, par * 128 + 64, (1 - par) * 128
     o0, o1 = (1 - par) * 128, (1 - par) * 128 + 64
@@ -107,30 +104,43 @@
         move(m, 1, rest, 128, Y_C, yd(1)).wait_recv()
         move(m, 2, rest, 128, Y_C + 1, yd(-1)).wait_recv()
 
-    def x_sends(m, role):
+    def x_up(m, role):
         move(m, role, q0, 64, XQ + 2 * (role - 3), xd(1)).start()
+
+    def x_down(m, role):
         move(m, role, q1, 64, XQ + 2 * (role - 3) + 1, xd(-1)).start()
 
     def y_far(m):
         move(m, 3, q0, 64, Y2, yd(1)).wait_recv()
+        x_up(m, 3)
         move(m, 3, q1, 64, Y2 + 1, yd(-1)).wait_recv()
-        x_sends(m, 3)
+        x_down(m, 3)
         z_source(m, 3)
 
-    def z_pass(m, k):
-        move(m, 4 + k, q0, 64, ZU + k, zd(1)).wait_recv()
-
-        @pl.when(j < 3)
-        def _():
-            move(m, 4 + k, q0, 64, ZU + k, zd(1)).start()
-
-        move(m, 4 + k, q1, 64, ZD + k, zd(-1)).wait_recv()
-
-        @pl.when(j > 0)
-        def _():
-            move(m, 4 + k, q1, 64, ZD + k, zd(-1)).start()
-
-        x_sends(m, 4 + k)
+    def z_step(n):
+        up, down = n - 2 * j, n - 2 * (3 - j)
+
+        @pl.when(jnp.logical_and(up >= 0, up < 8))
+        def _():
+            m, k = up // 4, up % 4
+            move(m, 4 + k, q0, 64, ZU + k, zd(1)).wait_recv()
+
+            @pl.when(j < 3)
+            def _():
+                move(m, 4 + k, q0, 64, ZU + k, zd(1)).start()
+
+            x_up(m, 4 + k)
+
+        @pl.when(jnp.logical_and(down >= 0, down < 8))
+        def _():
+            m, k = down // 4, down % 4
+            move(m, 4 + k, q1, 64, ZD + k, zd(-1)).wait_recv()
+
+            @pl.when(j > 0)
+            def _():
+                move(m, 4 + k, q1, 64, ZD + k, zd(-1)).start()
+
+            x_down(m, 4 + k)
 
     def x_wait(m, role):
         sem = XQ + 2 * (role - 3)
@@ -138,30 +148,26 @@
         move(m, role, o1, 64, sem + 1, xd(-1)).wait_recv()
 
     def to_sibling(role):
-        ref = wg.at[slot(role), mine]
-        return copy(ref, ref, SIB_W + role, sib)
-
-    theirs = pl.ds(pl.multiple_of((1 - c) * 256, 256), 256)
+        s = slot(role)
+        return copy(pg.at[0, s], ws.at[s], SIB_W + role, sib)
 
     def project(role):
-        ref = wg.at[slot(role), theirs]
-        copy(ref, ref, SIB_W + role, sib).wait_recv()
+        to_sibling(role).wait_recv()
         s = slot(role)
 
         @pl.loop(0, 4)
         def _(n):
             cols = pl.ds(pl.multiple_of(n * 256, 256), 256)
-            acc[:, cols] += jnp.dot(normed[s], wg[s, :, cols], preferred_element_type=f32)
-
-    to_sibling(0).start()
+            acc[:, cols] += jnp.dot(normed[s, c], pg[0, s, :, cols], preferred_element_type=f32) + jnp.dot(
+                normed[s, 1 - c], ws[s, :, cols], preferred_element_type=f32
+            )
+
     y_sends(0)
     z_source(0, 0)
+    to_sibling(0).start()
     id_copy = copy(idb.at[c], idb.at[c], SIB_I, sib)
     id_copy.start()
     hid_copy.wait()
-    head_copy.wait()
-    y_sends(1)
-    z_source(1, 0)
 
     @pl.loop(0, 32)
     def _(r):
@@ -169,42 +175,50 @@
         block = hid[at, :].astype(f32)
         inv = lax.rsqrt(jnp.mean(block * block, axis=-1, keepdims=True) + eps)
         out = (block * inv * t_gain[...]).astype(bf16)
-        for s in range(8):
-            normed[s, at, :] = out[:, s * 512 : (s + 1) * 512]
+        for s in range(16):
+            normed[s // 2, s % 2, at, :] = out[:, s * 256 : (s + 1) * 256]
 
     acc[...] = jnp.zeros_like(acc)
+    head_copy.wait()
+    z_step(0)
     y_quarters(0)
-    z_pass(0, 0)
+    y_sends(1)
+    z_source(1, 0)
+    z_step(1)
+    z_step(2)
     y_far(0)
+    z_step(3)
     y_quarters(1)
-    z_pass(1, 0)
-    z_pass(0, 1)
-    z_pass(0, 2)
+    z_step(4)
+    z_step(5)
     y_far(1)
     y_rest(0)
     to_sibling(1).start()
     to_sibling(2).start()
-    z_pass(0, 3)
     project(0)
-    z_pass(1, 1)
-    z_pass(1, 2)
+    z_step(6)
     project(1)
+    z_step(7)
     project(2)
     x_wait(0, 3)
     to_sibling(3).start()
+    z_step(8)
+    project(3)
     x_wait(0, 4)
     to_sibling(4).start()
-    z_pass(1, 3)
-    project(3)
+    z_step(9)
+    project(4)
     x_wait(0, 5)
     to_sibling(5).start()
-    project(4)
+    z_step(10)
+    project(5)
     x_wait(0, 6)
     to_sibling(6).start()
-    project(5)
+    z_step(11)
+    project(6)
     x_wait(0, 7)
     to_sibling(7).start()
-    project(6)
+    z_step(12)
     project(7)
 
     @pl.loop(0, 16)
@@ -218,6 +232,7 @@
     row_copy = copy(my_rows, my_rows, SIB_R, sib)
     sums[...] = jnp.zeros_like(sums)
     row_copy.start()
+    z_step(13)
     id_copy.wait_recv()
     row_copy.wait_recv()
     y_rest(1)
@@ -229,7 +244,7 @@
         def _(n):
             cols = pl.ds(pl.multiple_of(n * 256, 256), 256)
             got = lax.dot_general(
-                hg[s], rows[cols, :], (((1,), (1,)), ((), ())), preferred_element_type=f32
+                pg[1, s], rows[cols, :], (((1,), (1,)), ((), ())), preferred_element_type=f32
             )
             t = jnp.tanh(got * (1.0 / cap))
             e = jnp.exp(t * cap)
@@ -423,7 +438,7 @@
         in_specs=[hbm, vmem, vmem, vmem, vmem, hbm, vmem],
         out_specs=(vmem, vmem),
         scratch_shapes=[
-            V((512, 4096), bf16), V((8, 512, 512), bf16), V((8, 512, 1024), bf16), V((8, 256, 1024), bf16),
+            V((512, 4096), bf16), V((8, 2, 512, 256), bf16), V((2, 8, 256, 1024), bf16), V((8, 256, 1024), bf16),
             V((512, 1024), f32), V((1024, 1024), bf16), V((8, 256, 1024), f32), V((8, 256, 1024), f32),
             V((256, 1024), bf16), V((8, 256, 1024), bf16),
             V((8, 64, 512), bf16), V((8, 64, 512), bf16), V((8, 64, 512), bf16), V((8, 64, 512), bf16),

time: 297 us -> 137 us (0.46)
  Pallas kernels: 290 us -> 130 us
    pallas_call x1, Pallas kernels: 290 us -> 130 us  [shards(): pl.pallas_call(kernel, out_shape=(jax.ShapeDtypeStruct((4, 512), f32), ja...]
where the time goes in v2:
time: 137 us; the launch traced here: 136 us
  Pallas kernels  130 us (95%)
  local copies, waits for them, and re-layouts  4.99 us (4%)
    pallas_call x1, Pallas kernels, shards(): pl.pallas_call(kernel, out_shape=(jax.ShapeDtypeStruct((4, 512), f32), ja...  130 us
    unnamed x2, local copies, waits for them, and re-layouts  3.6 us

profile of v2, /device:TPU:2, one launch (start us, length us, event | category | flops | bytes accessed | tf_op | source)
XLA Modules:
  0.0 135.7 jit_solution(8568172738437139604)
XLA Ops:
  0.6 1.4 %broadcast_in_dim.12.scale = bf16[256,1]{1,0:T(8,128)(2,1)} reshape(bf16[256]{0:T(256)(128)(2,1)} %param.10) | data formatting | bytes 1024 | tf_op jit(solution)/shard_map/broadcast_in_dim | solution.py:456
  2.0 130.1 %shard_map.86 = (f32[4,512]{1,0:T(4,128)}, f32[4,64,1024]{2,1,0:T(8,128)}) custom-call(bf16[512,4096]{1,0:T(8,128)(2,1)} %hidden.1, f32[1,4096]{1,0:T(1,128)} %bitcast.6, bf16[256,1024]{1,0:T(8,128)(2,1)} %weight.1, bf16[256,1]{1,0:T(8,128)(2,1)} %broadcast_in_dim.12.scale, f32[1,1024]{1,0:T(1,128)} %bitcast.9, bf16[256,1024]{1,0:T(8,128)(2,1)} %bitcast.5, ...), custom_call_target="tpu_custom_call" | custom-call | tf_op jit(solution)/shard_map/pallas_call | solution.py:435
  132.1 1.3 copy.12
  133.4 2.3 %copy.13 = f32[4,64,1024]{2,1,0:T(8,128)} copy(f32[4,64,1024]{2,1,0:T(8,128)} %get-tuple-element.9) | data formatting | bytes 2097152

commit v3 on v0

v3 whole, which is shorter than its diff:
```python
import functools

import jax
import jax.numpy as jnp
from jax import lax
from jax.experimental import pallas as pl
from jax.experimental.pallas import tpu as pltpu
from jax.sharding import PartitionSpec as P

MESH = pl.DeviceIdType.MESH
f32, bf16 = jnp.float32, jnp.bfloat16
eps = 1e-05
cap = 30.0
loss_scale = 0.0625

Y_A, Y_B, Y_C, Y2, ZU, ZD, XQ = 0, 2, 4, 6, 8, 16, 24
GATHER = 44
SIB_W, SIB_R, SIB_S, SIB_I = 88, 96, 97, 98
RS = 99
A2, A1M, A1A, B2, B1M, B1A, S2A, S2B, S3, GZ, GX = 0, 8, 16, 24, 26, 28, 30, 33, 36, 43, 46
SUM = 58
N_SEM = RS + 2 * SUM
WIDTH = (384, 128)
A_COL = (0, WIDTH[0])
B_COL = (1024 - WIDTH[0], WIDTH[0] + WIDTH[1])


def kernel(
    hidden, t_gain, weight, scale, d_gain, heads, ids,
    loss_out, grad_out,
    hid, normed, pg, ws, acc, rows, tb, eb, dl, idb, sums, lsem, ss, rs, *parts,
):
    half_parts = len(parts) // 2
    parts = (parts[:half_parts], parts[half_parts:])
    dp, fs = lax.axis_index("dp"), lax.axis_index("fsdp")
    x, y, c = dp % 4, fs // 4, fs % 2
    h, j = (fs // 2) % 2, dp // 4
    z = h * 4 + j
    par = x % 2

    def dev(px, py, pz, pc=None):
        px, py, pz = (px + 4) % 4, (py + 4) % 4, (pz + 8) % 8
        return {"dp": (pz % 4) * 4 + px, "fsdp": (py * 2 + pz // 4) * 2 + (c if pc is None else pc)}

    sib = dev(x, y, z, 1 - c)
    xd = lambda d: dev(x + d, y, z)
    yd = lambda d: dev(x, y + d, z)
    zd = lambda d: dev(x, y, z + d)

    def copy(src, dst, sem, to):
        return pltpu.make_async_remote_copy(
            src_ref=src, dst_ref=dst, send_sem=ss.at[sem], recv_sem=rs.at[sem], device_id=to, device_id_type=MESH
        )

    hid_copy = pltpu.make_async_copy(hidden, hid, lsem.at[0])
    hid_copy.start()
    own = y * 2 + h
    head_copy = pltpu.make_async_copy(heads, pg.at[1, own], lsem.at[1])
    head_copy.start()

    barrier = pltpu.get_barrier_semaphore()
    everyone = [sib] + [xd(d) for d in (1, 2, 3)] + [yd(d) for d in (1, 2, 3)] + [zd(d) for d in range(1, 8)]
    for to in everyone:
        pl.semaphore_signal(barrier, inc=1, device_id=to, device_id_type=MESH)

    on_diagonal = lax.broadcasted_iota(jnp.int32, (256, 256), 0) == lax.broadcasted_iota(jnp.int32, (256, 256), 1)
    diagonal = jnp.where(on_diagonal, scale[...].astype(f32)[None, :], 0.0).astype(bf16)
    pg[0, own] = jnp.dot(diagonal, weight[...], preferred_element_type=f32).astype(bf16)
    idb[pl.ds(c, 1)] = ids[...][None]
    pl.semaphore_wait(barrier, len(everyone))

    def slot(role):
        off = jnp.where(role % 4 == 1, 3, jnp.where(role % 4 == 2, 1, jnp.where(role % 4 == 3, 2, 0)))
        return ((y + off) % 4) * 2 + jnp.where(role < 4, h, 1 - h)

    def piece(m, role, start, count):
        return pg.at[m, slot(role), pl.ds(pl.multiple_of(start, 32), count)]

    q0, q1, rest = par * 128, par * 128 + 64, (1 - par) * 128
    o0, o1 = (1 - par) * 128, (1 - par) * 128 + 64

    def move(m, role, start, count, sem, to):
        ref = piece(m, role, start, count)
        return copy(ref, ref, m * GATHER + sem, to)

    def y_send(m, sem):
        plus, minus, count = {Y_A: (q0, q1, 64), Y_B: (q1, q0, 64), Y_C: (rest, rest, 128)}[sem]
        move(m, 0, plus, count, sem, yd(1)).start()
        move(m, 0, minus, count, sem + 1, yd(-1)).start()

    def z_up(m, k, half):
        return move(m, k, q0 + 32 * half, 32, ZU + 2 * (k % 4) + half, zd(1))

    def z_down(m, k, half):
        return move(m, k, q1 + 32 * half, 32, ZD + 2 * (k % 4) + half, zd(-1))

    def y_sent(m, sem):
        move(m, 0, 0, 64, sem, yd(1)).wait_send()
        move(m, 0, 0, 64, sem + 1, yd(-1)).wait_send()

    def up_source(m, k):
        @pl.when(j == 3)
        def _():
            z_up(m, k, 0).start()
            z_up(m, k, 1).start()

    def down_source(m, k):
        @pl.when(j == 0)
        def _():
            z_down(m, k, 0).start()
            z_down(m, k, 1).start()

    def x_up(m, role, half):
        return move(m, role, q0 + 32 * half, 32, XQ + 4 * (role - 3) + 2 * half, xd(1))

    def x_down(m, role, half):
        return move(m, role, q1 + 32 * half, 32, XQ + 4 * (role - 3) + 2 * half + 1, xd(-1))

    def y_first(m):
        move(m, 1, q0, 64, Y_A, yd(1)).wait_recv()
        move(m, 1, q0, 64, Y2, yd(1)).start()
        up_source(m, 1)
        move(m, 2, q1, 64, Y_A + 1, yd(-1)).wait_recv()
        move(m, 2, q1, 64, Y2 + 1, yd(-1)).start()
        down_source(m, 2)

    def y_second(m):
        move(m, 1, q1, 64, Y_B, yd(1)).wait_recv()
        down_source(m, 1)
        move(m, 2, q0, 64, Y_B + 1, yd(-1)).wait_recv()
        up_source(m, 2)

    def y_rest(m):
        move(m, 1, rest, 128, Y_C, yd(1)).wait_recv()
        move(m, 2, rest, 128, Y_C + 1, yd(-1)).wait_recv()

    def y_far(m):
        move(m, 3, q0, 64, Y2, yd(1)).wait_recv()
        up_source(m, 3)
        x_up(m, 3, 0).start()
        x_up(m, 3, 1).start()
        move(m, 3, q1, 64, Y2 + 1, yd(-1)).wait_recv()
        down_source(m, 3)
        x_down(m, 3, 0).start()
        x_down(m, 3, 1).start()

    def z_piece(i, first):
        q = i // 2
        k = jnp.where(q < 2, 0, jnp.where(q < 5, q - 1, q - 4))
        k = jnp.where(k == 1, first, jnp.where(k == 2, 3 - first, k))
        return jnp.where(jnp.logical_or(q == 1, q >= 5), 1, 0), 4 + k, i % 2

    def z_step(n):
        up, down = n - 3 * j, n - 3 * (3 - j)

        @pl.when(jnp.logical_and(up >= 0, up < 16))
        def _():
            m, role, half = z_piece(up, 1)
            z_up(m, role, half).wait_recv()

            @pl.when(j < 3)
            def _():
                z_up(m, role, half).start()

            x_up(m, role, half).start()

        @pl.when(jnp.logical_and(down >= 0, down < 16))
        def _():
            m, role, half = z_piece(down, 2)
            z_down(m, role, half).wait_recv()

            @pl.when(j > 0)
            def _():
                z_down(m, role, half).start()

            x_down(m, role, half).start()

    def x_wait(m, role):
        for half in range(2):
            sem = XQ + 4 * (role - 3) + 2 * half
            move(m, role, o0 + 32 * half, 32, sem, xd(1)).wait_recv()
            move(m, role, o1 + 32 * half, 32, sem + 1, xd(-1)).wait_recv()

    def to_sibling(role):
        s = slot(role)
        return copy(pg.at[0, s], ws.at[s], SIB_W + role, sib)

    def project(role):
        to_sibling(role).wait_recv()
        s = slot(role)

        @pl.loop(0, 4)
        def _(n):
            cols = pl.ds(pl.multiple_of(n * 256, 256), 256)
            acc[:, cols] += jnp.dot(normed[s, c], pg[0, s, :, cols], preferred_element_type=f32) + jnp.dot(
                normed[s, 1 - c], ws[s, :, cols], preferred_element_type=f32
            )

    y_send(0, Y_A)
    up_source(0, 0)
    down_source(0, 0)
    to_sibling(0).start()
    id_copy = copy(idb.at[c], idb.at[c], SIB_I, sib)
    id_copy.start()
    head_copy.wait()
    up_source(1, 0)
    down_source(1, 0)
    acc[...] = jnp.zeros_like(acc)
    sums[...] = jnp.zeros_like(sums)
    hid_copy.wait()

    def norm(part):
        @pl.loop(part * 4, part * 4 + 4)
        def _(r):
            at = pl.ds(pl.multiple_of(r * 16, 16), 16)
            block = hid[at, :].astype(f32)
            inv = lax.rsqrt(jnp.mean(block * block, axis=-1, keepdims=True) + eps)
            out = (block * inv * t_gain[...]).astype(bf16)
            for s in range(16):
                normed[s // 2, s % 2, at, :] = out[:, s * 256 : (s + 1) * 256]

    norm(0)
    norm(1)
    y_sent(0, Y_A)
    y_send(0, Y_B)
    z_step(0)
    y_first(0)
    z_step(1)
    norm(2)
    z_step(2)
    y_sent(0, Y_B)
    y_send(1, Y_A)
    z_step(3)
    y_second(0)
    z_step(4)
    norm(3)
    z_step(5)
    y_far(0)
    y_sent(1, Y_A)
    y_send(1, Y_B)
    z_step(6)
    y_first(1)
    norm(4)
    z_step(7)
    y_sent(1, Y_B)
    y_send(0, Y_C)
    z_step(8)
    y_second(1)
    norm(5)
    z_step(9)
    z_step(10)
    y_far(1)
    norm(6)
    z_step(11)
    norm(7)
    z_step(12)
    y_rest(0)
    to_sibling(1).start()
    to_sibling(2).start()
    y_send(1, Y_C)
    z_step(13)
    x_wait(0, 3)
    to_sibling(3).start()
    project(0)
    z_step(14)
    x_wait(0, 4)
    to_sibling(4).start()
    project(1)
    z_step(15)
    project(2)
    z_step(16)
    project(3)
    z_step(17)
    project(4)
    z_step(18)
    z_step(19)
    x_wait(0, 5)
    to_sibling(5).start()
    x_wait(0, 6)
    to_sibling(6).start()
    z_step(20)
    project(5)
    z_step(21)
    project(6)
    x_wait(0, 7)
    to_sibling(7).start()
    z_step(22)
    project(7)

    @pl.loop(0, 16)
    def _(r):
        at = pl.ds(pl.multiple_of(r * 32, 32), 32)
        block = acc[at, :]
        inv = lax.rsqrt(jnp.mean(block * block, axis=-1, keepdims=True) + eps)
        rows[pl.ds(pl.multiple_of(c * 512 + r * 32, 32), 32), :] = (block * inv * d_gain[...]).astype(bf16)

    my_rows = rows.at[pl.ds(pl.multiple_of(c * 512, 512), 512)]
    row_copy = copy(my_rows, my_rows, SIB_R, sib)
    row_copy.start()
    z_step(23)
    z_step(24)
    id_copy.wait_recv()
    y_rest(1)
    for role in range(3, 8):
        x_wait(1, role)

    def score(n):
        cols = pl.ds(pl.multiple_of(n * 256, 256), 256)
        got = lax.dot_general(
            pg[1].reshape(2048, 1024), rows[cols, :], (((1,), (1,)), ((), ())), preferred_element_type=f32
        )
        tb[:, :, cols] = got.reshape(8, 256, 256)
        ids_at = idb[n // 2, :, pl.ds(pl.multiple_of((n % 2) * 256, 256), 256)]

        @pl.loop(0, 8)
        def _(b):
            card = lax.broadcasted_iota(jnp.int32, (64, 256), 0) + (b * 2 + c) * 64
            for k in range(4):
                part = slice(k * 64, (k + 1) * 64)
                t = jnp.tanh(tb[b, part, cols] * (1.0 / cap))
                e = jnp.exp(t * cap)
                tb[b, part, cols] = t
                eb[b, part, cols] = e
                hit = card == ids_at[k : k + 1, :]
                sums[c, k : k + 1, cols] += jnp.sum(e, axis=0, keepdims=True)
                sums[c, k + 4 : k + 5, cols] += jnp.sum(jnp.where(hit, t, 0.0), axis=0, keepdims=True)

    @pl.loop(0, 2)
    def _(n):
        score(c * 2 + n)

    row_copy.wait_recv()

    @pl.loop(0, 2)
    def _(n):
        score((1 - c) * 2 + n)

    my_sums = sums.at[c]
    sum_copy = copy(my_sums, my_sums, SIB_S, sib)
    sum_copy.start()
    sum_copy.wait_recv()
    totals = sums[0, 0:4, :] + sums[1, 0:4, :]
    mine_f = pl.ds(pl.multiple_of(c * 512, 512), 512)
    loss_out[...] = jnp.log(sums[0, 0:4, mine_f] + sums[1, 0:4, mine_f]) - cap * (
        sums[0, 4:8, mine_f] + sums[1, 4:8, mine_f]
    )
    sum_copy.wait_send()
    sums[c, 0:4, :] = 1.0 / totals

    def logits(b):
        @pl.loop(0, 4)
        def _(n):
            cols = pl.ds(pl.multiple_of(n * 256, 256), 256)
            ids_at = idb[n // 2, :, pl.ds(pl.multiple_of((n % 2) * 256, 256), 256)]
            card = lax.broadcasted_iota(jnp.int32, (64, 256), 0) + (b * 2 + c) * 64
            for k in range(4):
                part = slice(k * 64, (k + 1) * 64)
                t = tb[b, part, cols]
                p = eb[b, part, cols] * sums[c, k : k + 1, cols]
                hit = card == ids_at[k : k + 1, :]
                p = jnp.where(hit, p - 1.0, p)
                dl[b, part, cols] = (p * ((1.0 - t * t) * loss_scale)).astype(bf16)

    head = lambda d: pl.ds(pl.multiple_of(((x + d + 4) % 4) * 64, 64), 64)
    my_head = head(0)
    strip = pl.ds(pl.multiple_of(j * 16, 16), 16)

    class Part:
        def __init__(self, q):
            self.w, self.a, self.b, self.base = WIDTH[q], A_COL[q], B_COL[q], RS + q * SUM
            (self.ga, self.gb, self.ra2, self.ra1m, self.ra1a, self.saa, self.rb2, self.rb1m, self.rb1a, self.sab,
             self.sa, self.sb, self.s2a, self.r2a, self.s2b, self.r2b, self.tt, self.s3, self.r3, self.fin) = parts[q]

        def send(self, src, dst, sem, to):
            return copy(src, dst, self.base + sem, to)

        def gradient(self, i):
            b0 = ((y + jnp.where(i == 0, 2, jnp.where(i == 1, 1, jnp.where(i == 2, 3, 0)))) % 4) * 2
            if self.base == RS:
                logits(b0)
                logits(b0 + 1)
            both = pl.ds(b0, 2)
            for col, out in ((self.a, self.ga), (self.b, self.gb)):
                g = jnp.dot(
                    dl[both].reshape(512, 1024), rows[:, col : col + self.w], preferred_element_type=f32
                ).reshape(2, 256, self.w)
                eb[both, :, col : col + self.w] = g
                out[both] = g.astype(bf16)
            for hp in range(2):
                s, b = 1 - 2 * hp, b0 + hp
                self.send(self.ga.at[b, head(2)], self.ra2.at[b], A2 + b, xd(s)).start()
                self.send(self.ga.at[b, head(-s)], self.ra1m.at[b], A1M + b, xd(-s)).start()

                @pl.when(i == 0)
                def _():
                    self.send(self.gb.at[b], self.rb2.at[hp], B2 + hp, yd(s)).start()

                @pl.when(i == 2 - hp)
                def _():
                    self.send(self.gb.at[b], self.rb1m.at[hp], B1M + hp, yd(-s)).start()

        def ride(self):
            for hp in range(2):
                s = 1 - 2 * hp
                b = ((y + s + 4) % 4) * 2 + hp
                self.send(self.sab.at[hp], self.rb2.at[hp], B2 + hp, yd(s)).wait_recv()
                for r in range(4):
                    at = slice(r * 64, (r + 1) * 64)
                    self.sab[hp, at, :] = (
                        eb[b, at, self.b : self.b + self.w] + self.rb2[hp, at, :].astype(f32)
                    ).astype(bf16)
                self.send(self.sab.at[hp], self.rb1a.at[hp], B1A + hp, yd(s)).start()

            @pl.loop(0, 8)
            def _(b):
                s = 1 - 2 * (b % 2)
                self.send(self.saa.at[b], self.ra2.at[b], A2 + b, xd(s)).wait_recv()
                self.saa[b] = (eb[b, head(s), self.a : self.a + self.w] + self.ra2[b].astype(f32)).astype(bf16)
                self.send(self.saa.at[b], self.ra1a.at[b], A1A + b, xd(s)).start()

        def first(self):
            for hp in range(2):
                s = 1 - 2 * hp
                self.send(self.sab.at[hp], self.rb1m.at[hp], B1M + hp, yd(-s)).wait_recv()
                self.send(self.sab.at[hp], self.rb1a.at[hp], B1A + hp, yd(s)).wait_recv()
                for r in range(4):
                    at = slice(r * 64, (r + 1) * 64)
                    self.sb[hp, at, :] = (
                        eb[y * 2 + hp, at, self.b : self.b + self.w]
                        + self.rb1m[hp, at, :].astype(f32)
                        + self.rb1a[hp, at, :].astype(f32)
                    )
            for d in (2, 1, 3):
                self.s2b[d - 1] = self.sb[:, head(d), :].astype(bf16)
                self.send(self.s2b.at[d - 1], self.r2b.at[d - 1], S2B + d - 1, xd(d)).start()

            @pl.loop(0, 8)
            def _(b):
                s = 1 - 2 * (b % 2)
                self.send(self.saa.at[b], self.ra1m.at[b], A1M + b, xd(-s)).wait_recv()
                self.send(self.saa.at[b], self.ra1a.at[b], A1A + b, xd(s)).wait_recv()
                self.sa[b] = (
                    eb[b, my_head, self.a : self.a + self.w] + self.ra1m[b].astype(f32) + self.ra1a[b].astype(f32)
                )

            for d in (2, 1, 3):
                self.s2a[d - 1] = self.sa[pl.ds(((y + d) % 4) * 2, 2)].astype(bf16)
                self.send(self.s2a.at[d - 1], self.r2a.at[d - 1], S2A + d - 1, yd(d)).start()

        def second(self):
            w = self.w
            for d in range(3):
                self.send(self.s2b.at[d], self.r2b.at[d], S2B + d, xd(d + 1)).wait_recv()
            self.tt[:, :, w:] = (
                self.sb[:, my_head, :]
                + self.r2b[0].astype(f32) + self.r2b[1].astype(f32) + self.r2b[2].astype(f32)
            )
            for d in range(3):
                self.send(self.s2a.at[d], self.r2a.at[d], S2A + d, yd(d + 1)).wait_recv()
            self.tt[:, :, :w] = (
                self.sa[pl.ds(y * 2, 2)]
                + self.r2a[0].astype(f32) + self.r2a[1].astype(f32) + self.r2a[2].astype(f32)
            )
            self.s3[...] = self.tt[...].astype(bf16)
            for d in (4, 3, 5, 2, 6, 1, 7):
                to = (z + d) % 8
                at = pl.ds(pl.multiple_of((to % 4) * 16, 16), 16)
                self.send(self.s3.at[to // 4, at], self.r3.at[d - 1], S3 + d - 1, zd(d)).start()

        def z_share(self, d):
            here = self.fin.at[x, strip]
            return self.send(here, here, GZ + d - 1, dev(x, y, h * 4 + (j + d) % 4))

        def x_share(self, e, d):
            here = self.fin.at[x, pl.ds(pl.multiple_of(((j + 4 - e) % 4) * 16, 16), 16)]
            return self.send(here, here, GX + 3 * e + d - 1, xd(d))

        def third(self):
            total = self.tt[h, strip, :]
            for d in (1, 7, 2, 6, 3, 5, 4):
                self.send(self.r3.at[d - 1], self.r3.at[d - 1], S3 + d - 1, zd(d)).wait_recv()
                total = total + self.r3[d - 1].astype(f32)
            self.fin[x, strip, :] = total.astype(bf16)
            for d in (2, 1, 3):
                self.z_share(d).start()
            for d in (2, 1, 3):
                self.x_share(0, d).start()

        def share(self):
            for e in (1, 3, 2):
                self.z_share(e).wait_recv()
                for d in (2, 1, 3):
                    self.x_share(e, d).start()
            self.store(x)

        def store(self, k):
            grad_out[k, :, self.a : self.a + self.w] = self.fin[k, :, : self.w]
            grad_out[k, :, self.b : self.b + self.w] = self.fin[k, :, self.w :]

        def finish(self):
            for d in (1, 3, 2):
                for e in (0, 1, 3, 2):
                    self.x_share(e, d).wait_recv()
                self.store((x + 4 - d) % 4)

        def sent(self):
            for b in range(8):
                for sem in (A2, A1M, A1A):
                    self.send(self.saa.at[b], self.ra2.at[b], sem + b, sib).wait_send()
            for hp in range(2):
                for sem in (B2, B1M, B1A):
                    self.send(self.sab.at[hp], self.rb2.at[hp], sem + hp, sib).wait_send()
            for d in range(3):
                self.send(self.s2a.at[d], self.r2a.at[d], S2A + d, sib).wait_send()
                self.send(self.s2b.at[d], self.r2b.at[d], S2B + d, sib).wait_send()
                self.z_share(d + 1).wait_send()
                for e in range(4):
                    self.x_share(e, d + 1).wait_send()
            for d in range(7):
                self.send(self.r3.at[d], self.r3.at[d], S3 + d, sib).wait_send()

    one, two = Part(0), Part(1)

    @pl.loop(0, 4)
    def _(i):
        one.gradient(i)

    @pl.loop(0, 4)
    def _(i):
        two.gradient(i)

    one.ride()
    two.ride()
    one.first()
    one.second()
    two.first()
    one.third()
    two.second()
    one.share()
    two.third()
    two.share()
    one.finish()
    two.finish()

    for m in range(2):
        for sem, count in ((Y_C, 128), (Y_C + 1, 128)):
            move(m, 0, 0, count, sem, yd(1)).wait_send()
        for sem in (Y2, Y2 + 1):
            move(m, 0, 0, 64, sem, yd(1)).wait_send()
        for sem in range(ZU, GATHER):
            move(m, 0, 0, 32, sem, yd(1)).wait_send()
    for role in range(8):
        to_sibling(role).wait_send()
    row_copy.wait_send()
    id_copy.wait_send()
    one.sent()
    two.sent()


def widen(loss, grad, loss_out, grad_out):
    loss_out[...] = loss[...]
    grad_out[...] = grad[...].astype(f32)


def part_scratch(w):
    shapes = (
        [((8, 256, w), bf16)] * 2 + [((8, 64, w), bf16)] * 4 + [((2, 256, w), bf16)] * 4
        + [((8, 64, w), f32), ((2, 256, w), f32)] + [((3, 2, 64, w), bf16)] * 4
        + [((2, 64, 2 * w), f32), ((2, 64, 2 * w), bf16), ((7, 16, 2 * w), bf16), ((4, 64, 2 * w), bf16)]
    )
    return [pltpu.VMEM(shape, kind) for shape, kind in shapes]


def shards(hidden, temporal_gain, in_weight, in_scale, depth_gain, head_weight, code_ids):
    vmem = pl.BlockSpec(memory_space=pltpu.VMEM)
    hbm = pl.BlockSpec(memory_space=pl.ANY)
    V = pltpu.VMEM
    loss, grad = pl.pallas_call(
        kernel,
        out_shape=(jax.ShapeDtypeStruct((4, 512), f32), jax.ShapeDtypeStruct((4, 64, 1024), bf16)),
        in_specs=[hbm, vmem, vmem, vmem, vmem, hbm, vmem],
        out_specs=(vmem, vmem),
        scratch_shapes=[
            V((512, 4096), bf16), V((8, 2, 512, 256), bf16), V((2, 8, 256, 1024), bf16), V((8, 256, 1024), bf16),
            V((512, 1024), f32), V((1024, 1024), bf16), V((8, 256, 1024), f32), V((8, 256, 1024), f32),
            V((8, 256, 1024), bf16), V((2, 4, 512), jnp.int32), V((2, 8, 1024), f32),
            pltpu.SemaphoreType.DMA((2,)), pltpu.SemaphoreType.DMA((N_SEM,)), pltpu.SemaphoreType.DMA((N_SEM,)),
            *part_scratch(WIDTH[0]), *part_scratch(WIDTH[1]),
        ],
        compiler_params=pltpu.CompilerParams(
            collective_id=0, has_side_effects=True, vmem_limit_bytes=63 * 2**20
        ),
    )(
        hidden, temporal_gain[None, :], in_weight, in_scale, depth_gain[None, :],
        head_weight.reshape(256, 1024), code_ids.T,
    )
    loss, grad = pl.pallas_call(
        widen,
        out_shape=(jax.ShapeDtypeStruct((4, 512), f32), jax.ShapeDtypeStruct((4, 64, 1024), f32)),
        in_specs=[vmem, vmem],
        out_specs=(vmem, vmem),
    )(loss, grad)
    return loss.T, grad


def solution(mesh):
    in_specs = (
        P(("dp", "fsdp"), None),
        P(),
        P("fsdp", None),
        P("fsdp"),
        P(),
        P(None, "fsdp", None),
        P(("dp", "fsdp"), None),
    )
    out_specs = (P(("dp", "fsdp"), None), P(None, "fsdp", None))
    return jax.shard_map(shards, mesh=mesh, in_specs=in_specs, out_specs=out_specs, check_vma=False)
```

time: 677 us -> 119 us (0.18)
  waiting for transfers between devices: 554 us -> 0 us
  Pallas kernels: 0 us -> 118 us
  blocking collectives: 61.1 us -> 0 us
  matrix products: 37.6 us -> 0 us
  between operations: 13.8 us -> 0.64 us
    psum x2 -> x0, waiting for transfers between devices: 333 us -> none  [the longest x1 171 us: shards(): totals, targets = lax.psum((exp_sums, target), 'fsdp')]
    all_gather x2 -> x0, waiting for transfers between devices: 220 us -> none  [the longest x1 145 us: shards(): group_rows = lax.all_gather(depth_rows, 'fsdp', axis=0, tiled=True)]
    pallas_call x0 -> x2, Pallas kernels: none -> 118 us  [the longest x1 116 us: shards(): pl.pallas_call(kernel, out_shape=(jax.ShapeDtypeStruct((4, 512), f32), ja...]
    all_gather x2 -> x0, blocking collectives: 61.1 us -> none  [the longest x1 35.2 us: shards(): row_scale = lax.all_gather(in_scale, 'fsdp', axis=0, tiled=True)]
    dot_general x3 -> x0, matrix products: 37.6 us -> none  [the longest x1 15.1 us: shards(): jnp.einsum('rkc,rd->kcd', dlogits, group_rows, preferred_element_type=jnp...]
  transfers between devices with their start and end apart: 4 -> 0, of which waited for: 4 -> 0; matrix products, arithmetic and copies ran while one was open for 1% -> 0% of each run, Pallas kernels for 0% -> 0%
where the time goes in v3:
time: 119 us
  Pallas kernels  118 us (99%)
    pallas_call x1, Pallas kernels, shards(): pl.pallas_call(kernel, out_shape=(jax.ShapeDtypeStruct((4, 512), f32), ja...  116 us

profile of v3, /device:TPU:2, one launch (start us, length us, event | category | flops | bytes accessed | tf_op | source)
XLA Modules:
  0.0 119.0 jit_solution(9317082353996631171)
XLA Ops:
  0.6 116.2 %shard_map.86 = (f32[4,512]{1,0:T(4,128)}, bf16[4,64,1024]{2,1,0:T(8,128)(2,1)}) custom-call(bf16[512,4096]{1,0:T(8,128)(2,1)} %hidden.1, f32[1,4096]{1,0:T(1,128)} %bitcast.6, bf16[256,1024]{1,0:T(8,128)(2,1)} %weight.1, bf16[256]{0:T(256)(128)(2,1)} %scale.1, f32[1,1024]{1,0:T(1,128)} %bitcast.8, bf16[256,1024]{1,0:T(8,128)(2,1)} %bitcast.5, s32[4,512]{1,0:T(4,128)} %bitcast.7), custom_call_target="tpu_custom_call" | custom-call | tf_op jit(solution)/shard_map/pallas_call | solution.py:578
  116.9 2.1 %shard_map.87 = (f32[4,512]{1,0:T(4,128)}, f32[4,64,1024]{2,1,0:T(8,128)}) custom-call(f32[4,512]{1,0:T(4,128)} %get-tuple-element.6.loss, bf16[4,64,1024]{2,1,0:T(8,128)(2,1)} %get-tuple-element.7.grad), custom_call_target="tpu_custom_call" | custom-call | tf_op jit(solution)/shard_map/pallas_call | solution.py:597

commit v4 on v3

--- a/solution.py
+++ b/solution.py
@@ -13,14 +13,15 @@
 cap = 30.0
 loss_scale = 0.0625
 
-Y_A, Y_B, Y_C, Y2, ZU, ZD, XQ = 0, 2, 4, 6, 8, 16, 24
-GATHER = 44
-SIB_W, SIB_R, SIB_S, SIB_I = 88, 96, 97, 98
-RS = 99
+Y_A, Y_B, Y_C, Y2, ZU, ZD, XQ = 0, 2, 4, 6, 8, 24, 40
+GATHER = 60
+SIB_W, SIB_R, SIB_S, SIB_I = 120, 128, 129, 130
+RS = 131
 A2, A1M, A1A, B2, B1M, B1A, S2A, S2B, S3, GZ, GX = 0, 8, 16, 24, 26, 28, 30, 33, 36, 43, 46
 SUM = 58
 N_SEM = RS + 2 * SUM
-WIDTH = (384, 128)
+HOP = 4
+WIDTH = (256, 256)
 A_COL = (0, WIDTH[0])
 B_COL = (1024 - WIDTH[0], WIDTH[0] + WIDTH[1])
 
@@ -74,7 +75,7 @@
         return ((y + off) % 4) * 2 + jnp.where(role < 4, h, 1 - h)
 
     def piece(m, role, start, count):
-        return pg.at[m, slot(role), pl.ds(pl.multiple_of(start, 32), count)]
+        return pg.at[m, slot(role), pl.ds(pl.multiple_of(start, 16), count)]
 
     q0, q1, rest = par * 128, par * 128 + 64, (1 - par) * 128
     o0, o1 = (1 - par) * 128, (1 - par) * 128 + 64
@@ -88,11 +89,11 @@
         move(m, 0, plus, count, sem, yd(1)).start()
         move(m, 0, minus, count, sem + 1, yd(-1)).start()
 
-    def z_up(m, k, half):
-        return move(m, k, q0 + 32 * half, 32, ZU + 2 * (k % 4) + half, zd(1))
-
-    def z_down(m, k, half):
-        return move(m, k, q1 + 32 * half, 32, ZD + 2 * (k % 4) + half, zd(-1))
+    def z_up(m, k, sub):
+        return move(m, k, q0 + 16 * sub, 16, ZU + 4 * (k % 4) + sub, zd(1))
+
+    def z_down(m, k, sub):
+        return move(m, k, q1 + 16 * sub, 16, ZD + 4 * (k % 4) + sub, zd(-1))
 
     def y_sent(m, sem):
         move(m, 0, 0, 64, sem, yd(1)).wait_send()
@@ -101,14 +102,14 @@
     def up_source(m, k):
         @pl.when(j == 3)
         def _():
-            z_up(m, k, 0).start()
-            z_up(m, k, 1).start()
+            for sub in range(4):
+                z_up(m, k, sub).start()
 
     def down_source(m, k):
         @pl.when(j == 0)
         def _():
-            z_down(m, k, 0).start()
-            z_down(m, k, 1).start()
+            for sub in range(4):
+                z_down(m, k, sub).start()
 
     def x_up(m, role, half):
         return move(m, role, q0 + 32 * half, 32, XQ + 4 * (role - 3) + 2 * half, xd(1))
@@ -145,35 +146,44 @@
         x_down(m, 3, 1).start()
 
     def z_piece(i, first):
-        q = i // 2
+        q = i // 4
         k = jnp.where(q < 2, 0, jnp.where(q < 5, q - 1, q - 4))
         k = jnp.where(k == 1, first, jnp.where(k == 2, 3 - first, k))
-        return jnp.where(jnp.logical_or(q == 1, q >= 5), 1, 0), 4 + k, i % 2
-
-    def z_step(n):
-        up, down = n - 3 * j, n - 3 * (3 - j)
-
-        @pl.when(jnp.logical_and(up >= 0, up < 16))
+        return jnp.where(jnp.logical_or(q == 1, q >= 5), 1, 0), 4 + k, i % 4
+
+    def z_one(n):
+        up, down = n - HOP * j, n - HOP * (3 - j)
+
+        @pl.when(jnp.logical_and(up >= 0, up < 32))
         def _():
-            m, role, half = z_piece(up, 1)
-            z_up(m, role, half).wait_recv()
+            m, role, sub = z_piece(up, 1)
+            z_up(m, role, sub).wait_recv()
 
             @pl.when(j < 3)
             def _():
-                z_up(m, role, half).start()
-
-            x_up(m, role, half).start()
-
-        @pl.when(jnp.logical_and(down >= 0, down < 16))
+                z_up(m, role, sub).start()
+
+            @pl.when(sub % 2 == 1)
+            def _():
+                x_up(m, role, sub // 2).start()
+
+        @pl.when(jnp.logical_and(down >= 0, down < 32))
         def _():
-            m, role, half = z_piece(down, 2)
-            z_down(m, role, half).wait_recv()
+            m, role, sub = z_piece(down, 2)
+            z_down(m, role, sub).wait_recv()
 
             @pl.when(j > 0)
             def _():
-                z_down(m, role, half).start()
-
-            x_down(m, role, half).start()
+                z_down(m, role, sub).start()
+
+            @pl.when(sub % 2 == 1)
+            def _():
+                x_down(m, role, sub // 2).start()
+
+    def z_step(n):
+        @pl.loop(2 * n, 2 * n + 2)
+        def _(i):
+            z_one(i)
 
     def x_wait(m, role):
         for half in range(2):
@@ -189,12 +199,9 @@
         to_sibling(role).wait_recv()
         s = slot(role)
 
-        @pl.loop(0, 4)
-        def _(n):
-            cols = pl.ds(pl.multiple_of(n * 256, 256), 256)
-            acc[:, cols] += jnp.dot(normed[s, c], pg[0, s, :, cols], preferred_element_type=f32) + jnp.dot(
-                normed[s, 1 - c], ws[s, :, cols], preferred_element_type=f32
-            )
+        acc[...] += jnp.dot(normed[s, c], pg[0, s], preferred_element_type=f32) + jnp.dot(
+            normed[s, 1 - c], ws[s], preferred_element_type=f32
+        )
 
     y_send(0, Y_A)
     up_source(0, 0)
@@ -210,14 +217,12 @@
     hid_copy.wait()
 
     def norm(part):
-        @pl.loop(part * 4, part * 4 + 4)
-        def _(r):
-            at = pl.ds(pl.multiple_of(r * 16, 16), 16)
-            block = hid[at, :].astype(f32)
-            inv = lax.rsqrt(jnp.mean(block * block, axis=-1, keepdims=True) + eps)
-            out = (block * inv * t_gain[...]).astype(bf16)
-            for s in range(16):
-                normed[s // 2, s % 2, at, :] = out[:, s * 256 : (s + 1) * 256]
+        at = pl.ds(part * 64, 64)
+        block = hid[at, :].astype(f32)
+        inv = lax.rsqrt(jnp.mean(block * block, axis=-1, keepdims=True) + eps)
+        out = (block * inv * t_gain[...]).astype(bf16)
+        for s in range(16):
+            normed[s // 2, s % 2, at, :] = out[:, s * 256 : (s + 1) * 256]
 
     norm(0)
     norm(1)
@@ -242,22 +247,18 @@
     y_first(1)
     norm(4)
     z_step(7)
+    z_step(8)
     y_sent(1, Y_B)
-    y_send(0, Y_C)
-    z_step(8)
     y_second(1)
     norm(5)
     z_step(9)
     z_step(10)
     y_far(1)
+    y_send(0, Y_C)
     norm(6)
     z_step(11)
     norm(7)
     z_step(12)
-    y_rest(0)
-    to_sibling(1).start()
-    to_sibling(2).start()
-    y_send(1, Y_C)
     z_step(13)
     x_wait(0, 3)
     to_sibling(3).start()
@@ -265,40 +266,40 @@
     z_step(14)
     x_wait(0, 4)
     to_sibling(4).start()
-    project(1)
     z_step(15)
-    project(2)
+    project(3)
+    y_send(1, Y_C)
     z_step(16)
-    project(3)
+    project(4)
     z_step(17)
-    project(4)
     z_step(18)
+    y_rest(0)
+    to_sibling(1).start()
+    to_sibling(2).start()
     z_step(19)
     x_wait(0, 5)
     to_sibling(5).start()
+    project(1)
     x_wait(0, 6)
     to_sibling(6).start()
     z_step(20)
+    project(2)
     project(5)
     z_step(21)
     project(6)
     x_wait(0, 7)
     to_sibling(7).start()
-    z_step(22)
     project(7)
 
-    @pl.loop(0, 16)
+    @pl.loop(0, 2)
     def _(r):
-        at = pl.ds(pl.multiple_of(r * 32, 32), 32)
-        block = acc[at, :]
+        block = acc[pl.ds(pl.multiple_of(r * 256, 256), 256), :]
         inv = lax.rsqrt(jnp.mean(block * block, axis=-1, keepdims=True) + eps)
-        rows[pl.ds(pl.multiple_of(c * 512 + r * 32, 32), 32), :] = (block * inv * d_gain[...]).astype(bf16)
+        rows[pl.ds(pl.multiple_of(c * 512 + r * 256, 256), 256), :] = (block * inv * d_gain[...]).astype(bf16)
 
     my_rows = rows.at[pl.ds(pl.multiple_of(c * 512, 512), 512)]
     row_copy = copy(my_rows, my_rows, SIB_R, sib)
     row_copy.start()
-    z_step(23)
-    z_step(24)
     id_copy.wait_recv()
     y_rest(1)
     for role in range(3, 8):
@@ -306,18 +307,15 @@
 
     def score(n):
         cols = pl.ds(pl.multiple_of(n * 256, 256), 256)
-        got = lax.dot_general(
-            pg[1].reshape(2048, 1024), rows[cols, :], (((1,), (1,)), ((), ())), preferred_element_type=f32
-        )
-        tb[:, :, cols] = got.reshape(8, 256, 256)
         ids_at = idb[n // 2, :, pl.ds(pl.multiple_of((n % 2) * 256, 256), 256)]
-
-        @pl.loop(0, 8)
-        def _(b):
+        for b in range(8):
+            got = lax.dot_general(
+                pg[1, b], rows[cols, :], (((1,), (1,)), ((), ())), preferred_element_type=f32
+            )
             card = lax.broadcasted_iota(jnp.int32, (64, 256), 0) + (b * 2 + c) * 64
             for k in range(4):
                 part = slice(k * 64, (k + 1) * 64)
-                t = jnp.tanh(tb[b, part, cols] * (1.0 / cap))
+                t = jnp.tanh(got[part] * (1.0 / cap))
                 e = jnp.exp(t * cap)
                 tb[b, part, cols] = t
                 eb[b, part, cols] = e
@@ -376,9 +374,8 @@
 
         def gradient(self, i):
             b0 = ((y + jnp.where(i == 0, 2, jnp.where(i == 1, 1, jnp.where(i == 2, 3, 0)))) % 4) * 2
-            if self.base == RS:
-                logits(b0)
-                logits(b0 + 1)
+            logits(b0)
+            logits(b0 + 1)
             both = pl.ds(b0, 2)
             for col, out in ((self.a, self.ga), (self.b, self.gb)):
                 g = jnp.dot(
@@ -387,17 +384,41 @@
                 eb[both, :, col : col + self.w] = g
                 out[both] = g.astype(bf16)
             for hp in range(2):
-                s, b = 1 - 2 * hp, b0 + hp
-                self.send(self.ga.at[b, head(2)], self.ra2.at[b], A2 + b, xd(s)).start()
-                self.send(self.ga.at[b, head(-s)], self.ra1m.at[b], A1M + b, xd(-s)).start()
+                b = b0 + hp
+                self.leave(b, hp)
 
                 @pl.when(i == 0)
                 def _():
-                    self.send(self.gb.at[b], self.rb2.at[hp], B2 + hp, yd(s)).start()
+                    self.far_b(b, hp)
 
                 @pl.when(i == 2 - hp)
                 def _():
-                    self.send(self.gb.at[b], self.rb1m.at[hp], B1M + hp, yd(-s)).start()
+                    self.near_b(b, hp)
+
+        def gradient_rest(self):
+            g = jnp.dot(
+                dl[...].reshape(2048, 1024), rows[:, self.a : self.a + 2 * self.w], preferred_element_type=f32
+            ).reshape(8, 256, 2 * self.w)
+            eb[:, :, self.a : self.a + 2 * self.w] = g
+            self.ga[...] = g[:, :, : self.w].astype(bf16)
+            self.gb[...] = g[:, :, self.w :].astype(bf16)
+            for hp in range(2):
+                s = 1 - 2 * hp
+                self.far_b(((y + 2) % 4) * 2 + hp, hp)
+                self.near_b(((y - s + 4) % 4) * 2 + hp, hp)
+            for b in range(8):
+                self.leave(b, b % 2)
+
+        def leave(self, b, hp):
+            s = 1 - 2 * hp
+            self.send(self.ga.at[b, head(2)], self.ra2.at[b], A2 + b, xd(s)).start()
+            self.send(self.ga.at[b, head(-s)], self.ra1m.at[b], A1M + b, xd(-s)).start()
+
+        def far_b(self, b, hp):
+            self.send(self.gb.at[b], self.rb2.at[hp], B2 + hp, yd(1 - 2 * hp)).start()
+
+        def near_b(self, b, hp):
+            self.send(self.gb.at[b], self.rb1m.at[hp], B1M + hp, yd(2 * hp - 1)).start()
 
         def ride(self):
             for hp in range(2):
@@ -525,19 +546,17 @@
     def _(i):
         one.gradient(i)
 
-    @pl.loop(0, 4)
-    def _(i):
-        two.gradient(i)
+    two.gradient_rest()
 
     one.ride()
     two.ride()
     one.first()
+    two.first()
     one.second()
-    two.first()
+    two.second()
     one.third()
-    two.second()
+    two.third()
     one.share()
-    two.third()
     two.share()
     one.finish()
     two.finish()
@@ -547,7 +566,9 @@
             move(m, 0, 0, count, sem, yd(1)).wait_send()
         for sem in (Y2, Y2 + 1):
             move(m, 0, 0, 64, sem, yd(1)).wait_send()
-        for sem in range(ZU, GATHER):
+        for sem in range(ZU, XQ):
+            move(m, 0, 0, 16, sem, yd(1)).wait_send()
+        for sem in range(XQ, GATHER):
             move(m, 0, 0, 32, sem, yd(1)).wait_send()
     for role in range(8):
         to_sibling(role).wait_send()

time: 119 us -> 110 us (0.924)
  Pallas kernels: 118 us -> 109 us
    pallas_call x1, Pallas kernels: 116 us -> 107 us  [shards(): pl.pallas_call(kernel, out_shape=(jax.ShapeDtypeStruct((4, 512), f32), ja...]
where the time goes in v4:
time: 110 us
  Pallas kernels  109 us (99%)
    pallas_call x1, Pallas kernels, shards(): pl.pallas_call(kernel, out_shape=(jax.ShapeDtypeStruct((4, 512), f32), ja...  107 us

profile of v4, /device:TPU:2, one launch (start us, length us, event | category | flops | bytes accessed | tf_op | source)
XLA Modules:
  0.0 109.5 jit_solution(8981005165768455851)
XLA Ops:
  0.6 106.8 %shard_map.86 = (f32[4,512]{1,0:T(4,128)}, bf16[4,64,1024]{2,1,0:T(8,128)(2,1)}) custom-call(bf16[512,4096]{1,0:T(8,128)(2,1)} %hidden.1, f32[1,4096]{1,0:T(1,128)} %bitcast.6, bf16[256,1024]{1,0:T(8,128)(2,1)} %weight.1, bf16[256]{0:T(256)(128)(2,1)} %scale.1, f32[1,1024]{1,0:T(1,128)} %bitcast.8, bf16[256,1024]{1,0:T(8,128)(2,1)} %bitcast.5, s32[4,512]{1,0:T(4,128)} %bitcast.7), custom_call_target="tpu_custom_call" | custom-call | tf_op jit(solution)/shard_map/pallas_call | solution.py:599
  107.4 2.1 %shard_map.87 = (f32[4,512]{1,0:T(4,128)}, f32[4,64,1024]{2,1,0:T(8,128)}) custom-call(f32[4,512]{1,0:T(4,128)} %get-tuple-element.6.loss, bf16[4,64,1024]{2,1,0:T(8,128)(2,1)} %get-tuple-element.7.grad), custom_call_target="tpu_custom_call" | custom-call | tf_op jit(solution)/shard_map/pallas_call | solution.py:618

commit v5 on v4

--- a/solution.py
+++ b/solution.py
@@ -29,7 +29,7 @@
 def kernel(
     hidden, t_gain, weight, scale, d_gain, heads, ids,
     loss_out, grad_out,
-    hid, normed, pg, ws, acc, rows, tb, eb, dl, idb, sums, lsem, ss, rs, *parts,
+    wbuf, hid, normed, pg, ws, acc, rows, tb, eb, dl, idb, sums, lsem, ss, rs, *parts,
 ):
     half_parts = len(parts) // 2
     parts = (parts[:half_parts], parts[half_parts:])
@@ -53,20 +53,23 @@
             src_ref=src, dst_ref=dst, send_sem=ss.at[sem], recv_sem=rs.at[sem], device_id=to, device_id_type=MESH
         )
 
+    barrier = pltpu.get_barrier_semaphore()
+    everyone = [sib] + [xd(d) for d in (1, 2, 3)] + [yd(d) for d in (1, 2, 3)] + [zd(d) for d in range(1, 8)]
+    for to in everyone:
+        pl.semaphore_signal(barrier, inc=1, device_id=to, device_id_type=MESH)
+
+    weight_copy = pltpu.make_async_copy(weight, wbuf, lsem.at[2])
+    weight_copy.start()
     hid_copy = pltpu.make_async_copy(hidden, hid, lsem.at[0])
     hid_copy.start()
     own = y * 2 + h
     head_copy = pltpu.make_async_copy(heads, pg.at[1, own], lsem.at[1])
     head_copy.start()
 
-    barrier = pltpu.get_barrier_semaphore()
-    everyone = [sib] + [xd(d) for d in (1, 2, 3)] + [yd(d) for d in (1, 2, 3)] + [zd(d) for d in range(1, 8)]
-    for to in everyone:
-        pl.semaphore_signal(barrier, inc=1, device_id=to, device_id_type=MESH)
-
     on_diagonal = lax.broadcasted_iota(jnp.int32, (256, 256), 0) == lax.broadcasted_iota(jnp.int32, (256, 256), 1)
     diagonal = jnp.where(on_diagonal, scale[...].astype(f32)[None, :], 0.0).astype(bf16)
-    pg[0, own] = jnp.dot(diagonal, weight[...], preferred_element_type=f32).astype(bf16)
+    weight_copy.wait()
+    pg[0, own] = jnp.dot(diagonal, wbuf[...], preferred_element_type=f32).astype(bf16)
     idb[pl.ds(c, 1)] = ids[...][None]
     pl.semaphore_wait(barrier, len(everyone))
 
@@ -599,13 +602,13 @@
     loss, grad = pl.pallas_call(
         kernel,
         out_shape=(jax.ShapeDtypeStruct((4, 512), f32), jax.ShapeDtypeStruct((4, 64, 1024), bf16)),
-        in_specs=[hbm, vmem, vmem, vmem, vmem, hbm, vmem],
+        in_specs=[hbm, vmem, hbm, vmem, vmem, hbm, vmem],
         out_specs=(vmem, vmem),
         scratch_shapes=[
-            V((512, 4096), bf16), V((8, 2, 512, 256), bf16), V((2, 8, 256, 1024), bf16), V((8, 256, 1024), bf16),
+            V((256, 1024), bf16), V((512, 4096), bf16), V((8, 2, 512, 256), bf16), V((2, 8, 256, 1024), bf16), V((8, 256, 1024), bf16),
             V((512, 1024), f32), V((1024, 1024), bf16), V((8, 256, 1024), f32), V((8, 256, 1024), f32),
             V((8, 256, 1024), bf16), V((2, 4, 512), jnp.int32), V((2, 8, 1024), f32),
-            pltpu.SemaphoreType.DMA((2,)), pltpu.SemaphoreType.DMA((N_SEM,)), pltpu.SemaphoreType.DMA((N_SEM,)),
+            pltpu.SemaphoreType.DMA((3,)), pltpu.SemaphoreType.DMA((N_SEM,)), pltpu.SemaphoreType.DMA((N_SEM,)),
             *part_scratch(WIDTH[0]), *part_scratch(WIDTH[1]),
         ],
         compiler_params=pltpu.CompilerParams(

time: 110 us -> 109 us (level)
  no operation moved by 1% of the time
where the time goes in v5:
time: 109 us
  Pallas kernels  108 us (99%)
    pallas_call x1, Pallas kernels, shards(): pl.pallas_call(kernel, out_shape=(jax.ShapeDtypeStruct((4, 512), f32), ja...  106 us

profile of v5, /device:TPU:2, one launch (start us, length us, event | category | flops | bytes accessed | tf_op | source)
XLA Modules:
  0.0 109.1 jit_solution(677300420584681701)
XLA Ops:
  0.6 106.3 %shard_map.86 = (f32[4,512]{1,0:T(4,128)}, bf16[4,64,1024]{2,1,0:T(8,128)(2,1)}) custom-call(bf16[512,4096]{1,0:T(8,128)(2,1)} %hidden.1, f32[1,4096]{1,0:T(1,128)} %bitcast.6, bf16[256,1024]{1,0:T(8,128)(2,1)} %weight.1, bf16[256]{0:T(256)(128)(2,1)} %scale.1, f32[1,1024]{1,0:T(1,128)} %bitcast.8, bf16[256,1024]{1,0:T(8,128)(2,1)} %bitcast.5, s32[4,512]{1,0:T(4,128)} %bitcast.7), custom_call_target="tpu_custom_call" | custom-call | tf_op jit(solution)/shard_map/pallas_call | solution.py:602
  107.0 2.1 %shard_map.87 = (f32[4,512]{1,0:T(4,128)}, f32[4,64,1024]{2,1,0:T(8,128)}) custom-call(f32[4,512]{1,0:T(4,128)} %get-tuple-element.6.loss, bf16[4,64,1024]{2,1,0:T(8,128)(2,1)} %get-tuple-element.7.grad), custom_call_target="tpu_custom_call" | custom-call | tf_op jit(solution)/shard_map/pallas_call | solution.py:621

commit v6 on v5

--- a/solution.py
+++ b/solution.py
@@ -311,6 +311,7 @@
     def score(n):
         cols = pl.ds(pl.multiple_of(n * 256, 256), 256)
         ids_at = idb[n // 2, :, pl.ds(pl.multiple_of((n % 2) * 256, 256), 256)]
+        total, target = [0.0] * 4, [0.0] * 4
         for b in range(8):
             got = lax.dot_general(
                 pg[1, b], rows[cols, :], (((1,), (1,)), ((), ())), preferred_element_type=f32
@@ -323,8 +324,11 @@
                 tb[b, part, cols] = t
                 eb[b, part, cols] = e
                 hit = card == ids_at[k : k + 1, :]
-                sums[c, k : k + 1, cols] += jnp.sum(e, axis=0, keepdims=True)
-                sums[c, k + 4 : k + 5, cols] += jnp.sum(jnp.where(hit, t, 0.0), axis=0, keepdims=True)
+                total[k] += jnp.sum(e.reshape(8, 8, 256), axis=0)
+                target[k] += jnp.sum(jnp.where(hit, t, 0.0).reshape(8, 8, 256), axis=0)
+        for k in range(4):
+            sums[c, k : k + 1, cols] = jnp.sum(total[k], axis=0, keepdims=True)
+            sums[c, k + 4 : k + 5, cols] = jnp.sum(target[k], axis=0, keepdims=True)
 
     @pl.loop(0, 2)
     def _(n):

time: 109 us -> 108 us (level)
  no operation moved by 1% of the time
where the time goes in v6:
time: 108 us
  Pallas kernels  108 us (100%)
    pallas_call x1, Pallas kernels, shards(): pl.pallas_call(kernel, out_shape=(jax.ShapeDtypeStruct((4, 512), f32), ja...  106 us

profile of v6, /device:TPU:2, one launch (start us, length us, event | category | flops | bytes accessed | tf_op | source)
XLA Modules:
  0.0 108.2 jit_solution(11108822861564095660)
XLA Ops:
  0.6 105.5 %shard_map.86 = (f32[4,512]{1,0:T(4,128)}, bf16[4,64,1024]{2,1,0:T(8,128)(2,1)}) custom-call(bf16[512,4096]{1,0:T(8,128)(2,1)} %hidden.1, f32[1,4096]{1,0:T(1,128)} %bitcast.6, bf16[256,1024]{1,0:T(8,128)(2,1)} %weight.1, bf16[256]{0:T(256)(128)(2,1)} %scale.1, f32[1,1024]{1,0:T(1,128)} %bitcast.8, bf16[256,1024]{1,0:T(8,128)(2,1)} %bitcast.5, s32[4,512]{1,0:T(4,128)} %bitcast.7), custom_call_target="tpu_custom_call" | custom-call | tf_op jit(solution)/shard_map/pallas_call | solution.py:606
  106.1 2.1 %shard_map.87 = (f32[4,512]{1,0:T(4,128)}, f32[4,64,1024]{2,1,0:T(8,128)}) custom-call(f32[4,512]{1,0:T(4,128)} %get-tuple-element.6.loss, bf16[4,64,1024]{2,1,0:T(8,128)(2,1)} %get-tuple-element.7.grad), custom_call_target="tpu_custom_call" | custom-call | tf_op jit(solution)/shard_map/pallas_call | solution.py:625
